TPU v7x, 512 devices: a whole 4x8x8 slice. The times are simulated.
512 devices in a mesh: dp: 16 (over y, z_lo), ctx: 32 (over x, z_hi, core).
Axes of the slice: x: 4, y: 8, z: 8 (z_hi: 4, z_lo: 2; z = z_hi * 2 + z_lo), core: 2. Of those that a mesh axis runs over, the one named last changes fastest.
Arguments:
- queries: bfloat16 [8192, 12288], P('ctx', 'dp'), may hold values from -48 to 48
- latent: bfloat16 [8192, 576], P('ctx'), may hold values from -20 to 20
- grad_out: bfloat16 [8192, 8192], P('ctx', 'dp'), may hold values from -6 to 6
- doc_ids: int32 [8192], P('ctx'), may hold values from 0 to 31, never falling along the last dimension, each value on 1 to 1024 neighbouring positions
- up_key: bfloat16 [512, 8192], P(None, 'dp'), may hold values from -0.25 to 0.25
- up_value: bfloat16 [512, 8192], P(None, 'dp'), may hold values from -0.25 to 0.25
Outputs:
- grad_queries: bfloat16 [8192, 12288], P('ctx', 'dp')
- grad_latent: float32 [8192, 576], P('ctx')
- grad_up_key: float32 [512, 8192], P('ctx', 'dp')
- grad_up_value: float32 [512, 8192], P('ctx', 'dp')
Inputs may be any that keep to these rules, and one draw needn't show every extreme that they name: doc_ids never fall along the sequence; a document holds 1 to 1024 tokens, and one holds exactly 1024.
All inputs are finite; a program needn't handle non-finite values.
Results may differ from a plain program's by a relative error of at most 0.0071.
Values may be sent and summed in bfloat16 or wider, within the bound.
A program may use at most 128 MiB of HBM per device.

v0:
```python
import jax
import jax.numpy as jnp
from jax import lax
from jax.sharding import PartitionSpec as P

LAT = 512
ROPE = 64
NOPE = 128
VDIM = 128
WIN = 4


def shortened(shard):
    return jax.tree.map(lambda a: a.astype(jnp.bfloat16) if a.dtype == jnp.float32 else a, shard)


def shifted(shard, axis, by):
    length = lax.axis_size(axis)
    pairs = [(i, i + by) for i in range(length) if 0 <= i + by < length]
    return lax.ppermute(shard, axis, pairs)


def passed_along(block, axis, distance):
    devices = range(lax.axis_size(axis))
    route = [((i - distance) % len(devices), i) for i in devices]
    return lax.ppermute(block, axis, route)


def block_scores(query_nope, query_rope, key_nope, key_rope, score_scale):
    nope_part = jnp.einsum("ihd,jhd->hij", query_nope, key_nope, preferred_element_type=jnp.float32)
    rope_part = jnp.einsum("ihd,jd->hij", query_rope, key_rope, preferred_element_type=jnp.float32)
    return score_scale * (nope_part + rope_part)


def block_allowed(my_docs, my_positions, key_docs, owner_index, row_count):
    key_positions = owner_index * row_count + jnp.arange(row_count, dtype=jnp.int32)
    same_doc = my_docs[:, None] == key_docs[None, :]
    causal = key_positions[None, :] <= my_positions[:, None]
    return same_doc & causal & (owner_index >= 0)


def add_tuple(first, second):
    return tuple((left + right for left, right in zip(first, second)))


def forward_first(packet):
    return jax.tree.map(
        lambda part, own: part.astype(own.dtype), shifted(shortened(packet), "ctx", 1), packet
    )


def forward_again(packet):
    return jax.tree.map(
        lambda part, own: part.astype(own.dtype), shifted(shortened(packet), "ctx", 1), packet
    )


def grads_along(carried):
    return passed_along(carried, "ctx", 1)


def grads_home(carried, reach):
    return passed_along(carried, "ctx", -reach)


def shards(queries, latent, grad_out, doc_ids, up_key, up_value):
    rows_here = queries.shape[0]
    head_count = up_key.shape[1] // NOPE
    score_scale = (NOPE + ROPE) ** (-0.5)
    highest = lax.Precision.HIGHEST
    my_index = lax.axis_index("ctx")
    query_split = queries.reshape(rows_here, head_count, NOPE + ROPE)
    query_nope = query_split[:, :, :NOPE]
    query_rope = query_split[:, :, NOPE:]
    latent_part = latent[:, :LAT]
    rope_key = latent[:, LAT:]
    key_up_wide = up_key.astype(jnp.float32)
    value_up_wide = up_value.astype(jnp.float32)
    keys_made = jnp.dot(latent[:, :LAT], up_key, preferred_element_type=jnp.float32).astype(
        jnp.bfloat16
    )
    values_made = jnp.dot(latent[:, :LAT], up_value, preferred_element_type=jnp.float32).astype(
        jnp.bfloat16
    )
    grad_rows = grad_out.reshape(rows_here, head_count, VDIM)
    my_positions = my_index * rows_here + jnp.arange(rows_here, dtype=jnp.int32)

    def stats_update(running, key_block, owner_index):
        keys_in, values_in, rope_in, docs_in = key_block
        allowed = block_allowed(doc_ids, my_positions, docs_in, owner_index, rows_here)
        row_max, row_total, weighted = running
        scores = block_scores(
            query_nope,
            query_rope,
            keys_in.reshape(rows_here, head_count, NOPE),
            rope_in,
            score_scale,
        )
        scores = jnp.where(allowed[None], scores, -jnp.inf)
        new_max = jnp.maximum(row_max, jnp.max(scores, axis=2))
        prob_rows = jnp.where(allowed[None], jnp.exp(scores - new_max[:, :, None]), 0.0)
        grad_probs = jnp.einsum(
            "ihd,jhd->hij",
            grad_rows,
            values_in.reshape(rows_here, head_count, VDIM),
            preferred_element_type=jnp.float32,
        )
        factor = jnp.exp(row_max - new_max)
        return (
            new_max,
            row_total * factor + jnp.sum(prob_rows, axis=2),
            weighted * factor + jnp.sum(prob_rows * grad_probs, axis=2),
        )

    own_block = (keys_made, values_made, rope_key, doc_ids)
    stored = [own_block]
    packets = [own_block]
    lowest = jnp.full((head_count, rows_here), -jnp.inf, jnp.float32)
    zero_stats = jnp.zeros((head_count, rows_here), jnp.float32)
    running = stats_update((lowest, zero_stats, zero_stats), own_block, my_index)
    packet = own_block
    for hop_count in range(1, WIN + 1):
        packet = forward_first(packet)
        packets.append(packet)
        key_block = packet
        stored.append(key_block)
        running = stats_update(running, key_block, my_index - hop_count)
    row_max, row_total, weighted = running
    row_lse = row_max + jnp.log(row_total)
    row_delta = weighted / row_total

    def grad_partials(key_block, owner_index):
        keys_in, values_in, rope_in, docs_in = key_block
        allowed = block_allowed(doc_ids, my_positions, docs_in, owner_index, rows_here)
        keys_heads = keys_in.reshape(rows_here, head_count, NOPE)
        scores = block_scores(query_nope, query_rope, keys_heads, rope_in, score_scale)
        prob_rows = jnp.where(allowed[None], jnp.exp(scores - row_lse[:, :, None]), 0.0)
        grad_probs = jnp.einsum(
            "ihd,jhd->hij",
            grad_rows,
            values_in.reshape(rows_here, head_count, VDIM),
            preferred_element_type=jnp.float32,
        )
        grad_scores = (score_scale * prob_rows * (grad_probs - row_delta[:, :, None])).astype(
            jnp.bfloat16
        )
        prob_low = prob_rows.astype(jnp.bfloat16)
        dq_nope = jnp.einsum(
            "hij,jhd->ihd", grad_scores, keys_heads, preferred_element_type=jnp.float32
        )
        dq_rope = jnp.einsum(
            "hij,jd->ihd", grad_scores, rope_in, preferred_element_type=jnp.float32
        )
        dk_nope = jnp.einsum(
            "hij,ihd->jhd", grad_scores, query_nope, preferred_element_type=jnp.float32
        ).reshape(rows_here, head_count * NOPE)
        dk_rope = jnp.einsum(
            "hij,ihd->jd", grad_scores, query_rope, preferred_element_type=jnp.float32
        )
        dv_rows = jnp.einsum(
            "hij,ihd->jhd", prob_low, grad_rows, preferred_element_type=jnp.float32
        ).reshape(rows_here, head_count * VDIM)
        return (dq_nope, dq_rope, dk_nope, dk_rope, dv_rows)

    def to_travel(partials):
        dk_nope, dk_rope, dv_rows = (partials[2], partials[3], partials[4])
        return ((dk_nope, dk_rope, dv_rows), None)

    own_part = grad_partials(own_block, my_index)
    dq_nope = own_part[0]
    dq_rope = own_part[1]
    own_travel, weight_acc = to_travel(own_part)
    packet = own_block
    carried = own_travel
    for hop_count in range(1, WIN + 1):
        packet = forward_again(packet)
        partials = grad_partials(packet, my_index - hop_count)
        dq_nope = dq_nope + partials[0]
        dq_rope = dq_rope + partials[1]
        travel, piece = to_travel(partials)
        carried = add_tuple(grads_along(carried), travel)
    total = grads_home(carried, WIN)
    grad_queries = (
        jnp.concatenate([dq_nope, dq_rope], axis=2)
        .reshape(rows_here, head_count * (NOPE + ROPE))
        .astype(jnp.bfloat16)
    )
    grad_key_nope, grad_key_rope, grad_values = total
    both_grads = jnp.concatenate([grad_key_nope, grad_values], axis=1)
    latent_grad = jnp.dot(grad_key_nope, key_up_wide.T, precision=highest) + jnp.dot(
        grad_values, value_up_wide.T, precision=highest
    )
    local_grad = jnp.concatenate([latent_grad, grad_key_rope], axis=1)
    latent_rows = latent_part.astype(jnp.float32)
    weight_rows = lax.psum_scatter(
        jnp.dot(latent_rows.T, both_grads, precision=highest),
        "ctx",
        scatter_dimension=0,
        tiled=True,
    )
    grad_up_key = weight_rows[:, : head_count * NOPE]
    grad_up_value = weight_rows[:, head_count * NOPE :]
    grad_latent = lax.psum(local_grad, "dp")
    return (grad_queries, grad_latent, grad_up_key, grad_up_value)


def solution(mesh):
    placed = (
        P("ctx", "dp"),
        P("ctx", None),
        P("ctx", "dp"),
        P("ctx"),
        P(None, "dp"),
        P(None, "dp"),
    )
    return jax.shard_map(
        shards,
        mesh=mesh,
        in_specs=placed,
        out_specs=(P("ctx", "dp"), P("ctx", None), P("ctx", "dp"), P("ctx", "dp")),
        check_vma=False,
    )
```

profile of v0, /device:TPU:2, one launch (start us, length us, event | category | flops | bytes accessed | tf_op | source)
XLA Modules:
  0.0 468.1 jit_solution(15758723534035237217)
XLA Ops:
  11.5 6.2 %collective-permute-start.2 = (bf16[256,64]{0,1:T(8,128)(2,1)}, bf16[256,64]{0,1:T(8,128)(2,1)}, u32[]{:S(2)}, u32[]{:S(2)}) collective-permute-start(bf16[256,64]{0,1:T(8,128)(2,1)} %slice.22), channel_id=1, source_target_pairs={{0,1},{1,2},{2,3},{3,4},{4,5},{5,6},{6,7},{7,8},{8,9},{9,10},{10,1... | collective-permute-start | bytes 98312 | tf_op jit(solution)/shard_map/ppermute | solution.py:20
  23.9 7.4 %collective-permute-start.1 = (bf16[256,512]{1,0:T(8,128)(2,1)}, bf16[256,512]{1,0:T(8,128)(2,1)}, u32[]{:S(2)}, u32[]{:S(2)}) collective-permute-start(bf16[256,512]{1,0:T(8,128)(2,1)} %convolution_convert_fusion.1), channel_id=1, source_target_pairs={{0,1},{1,2},{2,3},{3,4},{4,5},{5,6},{6,7},{7,8},{8,9},{9,10},{10,1... | collective-permute-start | bytes 786440 | tf_op jit(solution)/shard_map/ppermute | solution.py:20
  34.9 6.1 %collective-permute-done.3 = s32[256]{0:T(256)S(1)} collective-permute-done((s32[256]{0:T(256)S(1)}, s32[256]{0:T(256)S(1)}, u32[]{:S(2)}, u32[]{:S(2)}) %collective-permute-start.3) | collective-permute-done | bytes 1056 | tf_op jit(solution)/shard_map/ppermute | solution.py:20
  42.9 6.0 %collective-permute-done.6 = s32[256]{0:T(256)S(1)} collective-permute-done((s32[256]{0:T(256)S(1)}, s32[256]{0:T(256)S(1)}, u32[]{:S(2)}, u32[]{:S(2)}) %collective-permute-start.6) | collective-permute-done | bytes 1056 | tf_op jit(solution)/shard_map/ppermute | solution.py:20
  50.9 5.8 %collective-permute-done.9 = s32[256]{0:T(256)S(1)} collective-permute-done((s32[256]{0:T(256)S(1)}, s32[256]{0:T(256)S(1)}, u32[]{:S(2)}, u32[]{:S(2)}) %collective-permute-start.9) | collective-permute-done | bytes 1056 | tf_op jit(solution)/shard_map/ppermute | solution.py:20
  59.0 3.0 multiply_reduce_fusion.4
  66.1 4.6 collective-permute-done.5
  73.9 5.0 %collective-permute-done.8 = bf16[256,64]{0,1:T(8,128)(2,1)S(1)} collective-permute-done((bf16[256,64]{0,1:T(8,128)(2,1)S(1)}, bf16[256,64]{0,1:T(8,128)(2,1)S(1)}, u32[]{:S(2)}, u32[]{:S(2)}) %collective-permute-start.8) | collective-permute-done | bytes 32800 | tf_op jit(solution)/shard_map/ppermute | solution.py:20
  82.1 5.0 %collective-permute-done.11 = bf16[256,64]{0,1:T(8,128)(2,1)S(1)} collective-permute-done((bf16[256,64]{0,1:T(8,128)(2,1)S(1)}, bf16[256,64]{0,1:T(8,128)(2,1)S(1)}, u32[]{:S(2)}, u32[]{:S(2)}) %collective-permute-start.11) | collective-permute-done | bytes 32800 | tf_op jit(solution)/shard_map/ppermute | solution.py:20
  95.1 8.2 %collective-permute-done.4 = bf16[256,512]{1,0:T(8,128)(2,1)} collective-permute-done((bf16[256,512]{1,0:T(8,128)(2,1)}, bf16[256,512]{1,0:T(8,128)(2,1)}, u32[]{:S(2)}, u32[]{:S(2)}) %collective-permute-start.4) | collective-permute-done | bytes 262176 | tf_op jit(solution)/shard_map/ppermute | solution.py:20
  111.8 6.0 %collective-permute-done.7 = bf16[256,512]{1,0:T(8,128)(2,1)} collective-permute-done((bf16[256,512]{1,0:T(8,128)(2,1)}, bf16[256,512]{1,0:T(8,128)(2,1)}, u32[]{:S(2)}, u32[]{:S(2)}) %collective-permute-start.7) | collective-permute-done | bytes 262176 | tf_op jit(solution)/shard_map/ppermute | solution.py:20
  126.6 6.2 %collective-permute-done.10 = bf16[256,512]{1,0:T(8,128)(2,1)} collective-permute-done((bf16[256,512]{1,0:T(8,128)(2,1)}, bf16[256,512]{1,0:T(8,128)(2,1)}, u32[]{:S(2)}, u32[]{:S(2)}) %collective-permute-start.10) | collective-permute-done | bytes 262176 | tf_op jit(solution)/shard_map/ppermute | solution.py:20
  152.4 5.5 %collective-permute-done.21 = f32[256,512]{0,1:T(8,128)S(1)} collective-permute-done((f32[256,512]{0,1:T(8,128)S(1)}, f32[256,512]{0,1:T(8,128)S(1)}, u32[]{:S(2)}, u32[]{:S(2)}) %collective-permute-start.21) | collective-permute-done | bytes 524320 | tf_op jit(solution)/shard_map/ppermute | solution.py:26
  159.9 11.6 %collective-permute-done.16 = f32[256,512]{0,1:T(8,128)S(1)} collective-permute-done((f32[256,512]{0,1:T(8,128)S(1)}, f32[256,512]{0,1:T(8,128)S(1)}, u32[]{:S(2)}, u32[]{:S(2)}) %collective-permute-start.16) | collective-permute-done | bytes 524320 | tf_op jit(solution)/shard_map/ppermute | solution.py:26
  176.2 10.4 %collective-permute-done.22 = f32[256,512]{0,1:T(8,128)S(1)} collective-permute-done((f32[256,512]{0,1:T(8,128)S(1)}, f32[256,512]{0,1:T(8,128)S(1)}, u32[]{:S(2)}, u32[]{:S(2)}) %collective-permute-start.22) | collective-permute-done | bytes 524320 | tf_op jit(solution)/shard_map/ppermute | solution.py:26
  188.6 11.7 %collective-permute-done.17 = f32[256,512]{0,1:T(8,128)S(1)} collective-permute-done((f32[256,512]{0,1:T(8,128)S(1)}, f32[256,512]{0,1:T(8,128)S(1)}, u32[]{:S(2)}, u32[]{:S(2)}) %collective-permute-start.17) | collective-permute-done | bytes 524320 | tf_op jit(solution)/shard_map/ppermute | solution.py:26
  204.9 10.6 %collective-permute-done.23 = f32[256,512]{0,1:T(8,128)S(1)} collective-permute-done((f32[256,512]{0,1:T(8,128)S(1)}, f32[256,512]{0,1:T(8,128)S(1)}, u32[]{:S(2)}, u32[]{:S(2)}) %collective-permute-start.23) | collective-permute-done | bytes 524320 | tf_op jit(solution)/shard_map/ppermute | solution.py:26
  217.4 11.7 %collective-permute-done.18 = f32[256,512]{0,1:T(8,128)S(1)} collective-permute-done((f32[256,512]{0,1:T(8,128)S(1)}, f32[256,512]{0,1:T(8,128)S(1)}, u32[]{:S(2)}, u32[]{:S(2)}) %collective-permute-start.18) | collective-permute-done | bytes 524320 | tf_op jit(solution)/shard_map/ppermute | solution.py:26
  233.7 11.4 %collective-permute-done.24 = f32[256,512]{0,1:T(8,128)S(1)} collective-permute-done((f32[256,512]{0,1:T(8,128)S(1)}, f32[256,512]{0,1:T(8,128)S(1)}, u32[]{:S(2)}, u32[]{:S(2)}) %collective-permute-start.24) | collective-permute-done | bytes 524320 | tf_op jit(solution)/shard_map/ppermute | solution.py:26
  247.5 28.9 %collective-permute-done.19 = f32[256,512]{0,1:T(8,128)S(1)} collective-permute-done((f32[256,512]{0,1:T(8,128)S(1)}, f32[256,512]{0,1:T(8,128)S(1)}, u32[]{:S(2)}, u32[]{:S(2)}) %collective-permute-start.19) | collective-permute-done | bytes 524320 | tf_op jit(solution)/shard_map/ppermute | solution.py:26
  276.6 3.5 collective-permute-start.20
  285.0 14.5 %collective-permute-done.20 = f32[256,512]{0,1:T(8,128)S(1)} collective-permute-done((f32[256,512]{0,1:T(8,128)S(1)}, f32[256,512]{0,1:T(8,128)S(1)}, u32[]{:S(2)}, u32[]{:S(2)}) %collective-permute-start.20) | collective-permute-done | bytes 524320 | tf_op jit(solution)/shard_map/ppermute | solution.py:26
  302.0 3.6 convolution_bitcast_fusion
  313.3 143.8 %all-reduce.2.cloned.1.call-done = f32[256,576]{1,0:T(8,128)} async-done(((f32[256,576]{1,0:T(8,128)}), f32[256,576]{1,0:T(8,128)}) %all-reduce.2.cloned.1.call-update) | async-done | bytes 589840 | tf_op jit(solution)/shard_map/psum | solution.py:203
  (193 shorter events, 114.7 us)
Async XLA Ops:
  8.0 449.1 %all-reduce.2.cloned.1.call-start = ((), (), s32[]{:S(2)}) async-start(), calls=%async_computation.1 | async-start | bytes 1310720 | tf_op jit(solution)/shard_map/psum | solution.py:203
  8.1 24.9 %collective-permute-start = (s32[256]{0:T(256)}, s32[256]{0:T(256)S(1)}, u32[]{:S(2)}, u32[]{:S(2)}) collective-permute-start(s32[256]{0:T(256)} %param.9), channel_id=1, source_target_pairs={{0,1},{1,2},{2,3},{3,4},{4,5},{5,6},{6,7},{7,8},{8,9},{9,10},{10,1... | collective-permute-start | bytes 3080 | tf_op jit(solution)/shard_map/ppermute | solution.py:20
  11.5 50.6 %collective-permute-start.2 = (bf16[256,64]{0,1:T(8,128)(2,1)}, bf16[256,64]{0,1:T(8,128)(2,1)}, u32[]{:S(2)}, u32[]{:S(2)}) collective-permute-start(bf16[256,64]{0,1:T(8,128)(2,1)} %slice.22), channel_id=1, source_target_pairs={{0,1},{1,2},{2,3},{3,4},{4,5},{5,6},{6,7},{7,8},{8,9},{9,10},{10,1... | collective-permute-start | bytes 98312 | tf_op jit(solution)/shard_map/ppermute | solution.py:20
  19.7 71.8 %collective-permute-start.12 = (bf16[256,512]{1,0:T(8,128)(2,1)}, bf16[256,512]{1,0:T(8,128)(2,1)}, u32[]{:S(2)}, u32[]{:S(2)}) collective-permute-start(bf16[256,512]{1,0:T(8,128)(2,1)} %convolution_convert_fusion), channel_id=1, source_target_pairs={{0,1},{1,2},{2,3},{3,4},{4,5},{5,6},{6,7},{7,8},{8,9},{9,10},{10,1... | collective-permute-start | bytes 786440 | tf_op jit(solution)/shard_map/ppermute | solution.py:20
  23.9 64.6 %collective-permute-start.1 = (bf16[256,512]{1,0:T(8,128)(2,1)}, bf16[256,512]{1,0:T(8,128)(2,1)}, u32[]{:S(2)}, u32[]{:S(2)}) collective-permute-start(bf16[256,512]{1,0:T(8,128)(2,1)} %convolution_convert_fusion.1), channel_id=1, source_target_pairs={{0,1},{1,2},{2,3},{3,4},{4,5},{5,6},{6,7},{7,8},{8,9},{9,10},{10,1... | collective-permute-start | bytes 786440 | tf_op jit(solution)/shard_map/ppermute | solution.py:20
  91.5 15.6 %collective-permute-start.13 = (bf16[256,512]{1,0:T(8,128)(2,1)}, bf16[256,512]{1,0:T(8,128)(2,1)}, u32[]{:S(2)}, u32[]{:S(2)}) collective-permute-start(bf16[256,512]{1,0:T(8,128)(2,1)} %collective-permute-done.12), channel_id=1, source_target_pairs={{0,1},{1,2},{2,3},{3,4},{4,5},{5,6},{6,7},{7,8},{8,9},{9,10},{10,1... | collective-permute-start | bytes 786440 | tf_op jit(solution)/shard_map/ppermute | solution.py:20
  107.1 14.9 %collective-permute-start.14 = (bf16[256,512]{1,0:T(8,128)(2,1)}, bf16[256,512]{1,0:T(8,128)(2,1)}, u32[]{:S(2)}, u32[]{:S(2)}) collective-permute-start(bf16[256,512]{1,0:T(8,128)(2,1)} %collective-permute-done.13), channel_id=1, source_target_pairs={{0,1},{1,2},{2,3},{3,4},{4,5},{5,6},{6,7},{7,8},{8,9},{9,10},{10,1... | collective-permute-start | bytes 786440 | tf_op jit(solution)/shard_map/ppermute | solution.py:20
  118.9 13.9 %collective-permute-start.10 = (bf16[256,512]{1,0:T(8,128)(2,1)}, bf16[256,512]{1,0:T(8,128)(2,1)}, u32[]{:S(2)}, u32[]{:S(2)}) collective-permute-start(bf16[256,512]{1,0:T(8,128)(2,1)} %collective-permute-done.7), channel_id=1, source_target_pairs={{0,1},{1,2},{2,3},{3,4},{4,5},{5,6},{6,7},{7,8},{8,9},{9,10},{10,1... | collective-permute-start | bytes 786440 | tf_op jit(solution)/shard_map/ppermute | solution.py:20
  122.0 18.8 %collective-permute-start.15 = (bf16[256,512]{1,0:T(8,128)(2,1)}, bf16[256,512]{1,0:T(8,128)(2,1)}, u32[]{:S(2)}, u32[]{:S(2)}) collective-permute-start(bf16[256,512]{1,0:T(8,128)(2,1)} %collective-permute-done.14), channel_id=1, source_target_pairs={{0,1},{1,2},{2,3},{3,4},{4,5},{5,6},{6,7},{7,8},{8,9},{9,10},{10,1... | collective-permute-start | bytes 786440 | tf_op jit(solution)/shard_map/ppermute | solution.py:20
  147.9 23.6 %collective-permute-start.16 = (f32[256,512]{0,1:T(8,128)S(1)}, f32[256,512]{0,1:T(8,128)S(1)}, u32[]{:S(2)}, u32[]{:S(2)}) collective-permute-start(f32[256,512]{0,1:T(8,128)S(1)} %bitcast.280), channel_id=1, source_target_pairs={{31,0},{0,1},{1,2},{2,3},{3,4},{4,5},{5,6},{6,7},{7,8},{8,9},{9,10... | collective-permute-start | bytes 1572872 | tf_op jit(solution)/shard_map/ppermute | solution.py:26
  150.1 23.8 %collective-permute-start.26 = (f32[256,64]{1,0:T(8,128)S(1)}, f32[256,64]{1,0:T(8,128)S(1)}, u32[]{:S(2)}, u32[]{:S(2)}) collective-permute-start(f32[256,64]{1,0:T(8,128)S(1)} %convolution_bitcast_fusion.20), channel_id=1, source_target_pairs={{31,0},{0,1},{1,2},{2,3},{3,4},{4,5},{5,6},{6,7},{7,8},{8,9},{9,10... | collective-permute-start | bytes 196616 | tf_op jit(solution)/shard_map/ppermute | solution.py:26
  157.9 28.7 %collective-permute-start.22 = (f32[256,512]{0,1:T(8,128)S(1)}, f32[256,512]{0,1:T(8,128)S(1)}, u32[]{:S(2)}, u32[]{:S(2)}) collective-permute-start(f32[256,512]{0,1:T(8,128)S(1)} %bitcast_add_fusion.3), channel_id=1, source_target_pairs={{31,0},{0,1},{1,2},{2,3},{3,4},{4,5},{5,6},{6,7},{7,8},{8,9},{9,10... | collective-permute-start | bytes 1572872 | tf_op jit(solution)/shard_map/ppermute | solution.py:26
  171.6 28.8 %collective-permute-start.17 = (f32[256,512]{0,1:T(8,128)S(1)}, f32[256,512]{0,1:T(8,128)S(1)}, u32[]{:S(2)}, u32[]{:S(2)}) collective-permute-start(f32[256,512]{0,1:T(8,128)S(1)} %bitcast_add_fusion.7), channel_id=1, source_target_pairs={{31,0},{0,1},{1,2},{2,3},{3,4},{4,5},{5,6},{6,7},{7,8},{8,9},{9,10... | collective-permute-start | bytes 1572872 | tf_op jit(solution)/shard_map/ppermute | solution.py:26
  174.3 28.4 %collective-permute-start.27 = (f32[256,64]{1,0:T(8,128)S(1)}, f32[256,64]{1,0:T(8,128)S(1)}, u32[]{:S(2)}, u32[]{:S(2)}) collective-permute-start(f32[256,64]{1,0:T(8,128)S(1)} %fusion.14), channel_id=1, source_target_pairs={{31,0},{0,1},{1,2},{2,3},{3,4},{4,5},{5,6},{6,7},{7,8},{8,9},{9,10... | collective-permute-start | bytes 196616 | tf_op jit(solution)/shard_map/ppermute | solution.py:26
  186.7 28.8 %collective-permute-start.23 = (f32[256,512]{0,1:T(8,128)S(1)}, f32[256,512]{0,1:T(8,128)S(1)}, u32[]{:S(2)}, u32[]{:S(2)}) collective-permute-start(f32[256,512]{0,1:T(8,128)S(1)} %bitcast_add_fusion.2), channel_id=1, source_target_pairs={{31,0},{0,1},{1,2},{2,3},{3,4},{4,5},{5,6},{6,7},{7,8},{8,9},{9,10... | collective-permute-start | bytes 1572872 | tf_op jit(solution)/shard_map/ppermute | solution.py:26
  200.4 28.8 %collective-permute-start.18 = (f32[256,512]{0,1:T(8,128)S(1)}, f32[256,512]{0,1:T(8,128)S(1)}, u32[]{:S(2)}, u32[]{:S(2)}) collective-permute-start(f32[256,512]{0,1:T(8,128)S(1)} %bitcast_add_fusion.6), channel_id=1, source_target_pairs={{31,0},{0,1},{1,2},{2,3},{3,4},{4,5},{5,6},{6,7},{7,8},{8,9},{9,10... | collective-permute-start | bytes 1572872 | tf_op jit(solution)/shard_map/ppermute | solution.py:26
  202.9 28.5 %collective-permute-start.28 = (f32[256,64]{1,0:T(8,128)S(1)}, f32[256,64]{1,0:T(8,128)S(1)}, u32[]{:S(2)}, u32[]{:S(2)}) collective-permute-start(f32[256,64]{1,0:T(8,128)S(1)} %fusion.95), channel_id=1, source_target_pairs={{31,0},{0,1},{1,2},{2,3},{3,4},{4,5},{5,6},{6,7},{7,8},{8,9},{9,10... | collective-permute-start | bytes 196616 | tf_op jit(solution)/shard_map/ppermute | solution.py:26
  215.5 29.6 %collective-permute-start.24 = (f32[256,512]{0,1:T(8,128)S(1)}, f32[256,512]{0,1:T(8,128)S(1)}, u32[]{:S(2)}, u32[]{:S(2)}) collective-permute-start(f32[256,512]{0,1:T(8,128)S(1)} %bitcast_add_fusion.1), channel_id=1, source_target_pairs={{31,0},{0,1},{1,2},{2,3},{3,4},{4,5},{5,6},{6,7},{7,8},{8,9},{9,10... | collective-permute-start | bytes 1572872 | tf_op jit(solution)/shard_map/ppermute | solution.py:26
  229.2 47.3 %collective-permute-start.19 = (f32[256,512]{0,1:T(8,128)S(1)}, f32[256,512]{0,1:T(8,128)S(1)}, u32[]{:S(2)}, u32[]{:S(2)}) collective-permute-start(f32[256,512]{0,1:T(8,128)S(1)} %bitcast_add_fusion.5), channel_id=1, source_target_pairs={{31,0},{0,1},{1,2},{2,3},{3,4},{4,5},{5,6},{6,7},{7,8},{8,9},{9,10... | collective-permute-start | bytes 1572872 | tf_op jit(solution)/shard_map/ppermute | solution.py:26
  231.8 48.3 %collective-permute-start.29 = (f32[256,64]{1,0:T(8,128)S(1)}, f32[256,64]{1,0:T(8,128)S(1)}, u32[]{:S(2)}, u32[]{:S(2)}) collective-permute-start(f32[256,64]{1,0:T(8,128)S(1)} %fusion.98), channel_id=1, source_target_pairs={{31,0},{0,1},{1,2},{2,3},{3,4},{4,5},{5,6},{6,7},{7,8},{8,9},{9,10... | collective-permute-start | bytes 196616 | tf_op jit(solution)/shard_map/ppermute | solution.py:26
  245.2 37.9 %collective-permute-start.25 = (f32[256,512]{0,1:T(8,128)S(1)}, f32[256,512]{0,1:T(8,128)S(1)}, u32[]{:S(2)}, u32[]{:S(2)}) collective-permute-start(f32[256,512]{0,1:T(8,128)S(1)} %bitcast_add_fusion), channel_id=1, source_target_pairs={{4,0},{5,1},{6,2},{7,3},{8,4},{9,5},{10,6},{11,7},{12,8},{13,9},{1... | collective-permute-start | bytes 1572872 | tf_op jit(solution)/shard_map/ppermute | solution.py:26
  276.6 23.0 %collective-permute-start.20 = (f32[256,512]{0,1:T(8,128)S(1)}, f32[256,512]{0,1:T(8,128)S(1)}, u32[]{:S(2)}, u32[]{:S(2)}) collective-permute-start(f32[256,512]{0,1:T(8,128)S(1)} %bitcast_add_fusion.4), channel_id=1, source_target_pairs={{4,0},{5,1},{6,2},{7,3},{8,4},{9,5},{10,6},{11,7},{12,8},{13,9},{1... | collective-permute-start | bytes 1572872 | tf_op jit(solution)/shard_map/ppermute | solution.py:26
  280.4 20.6 %collective-permute-start.30 = (f32[256,64]{1,0:T(8,128)S(1)}, f32[256,64]{1,0:T(8,128)S(1)}, u32[]{:S(2)}, u32[]{:S(2)}) collective-permute-start(f32[256,64]{1,0:T(8,128)S(1)} %fusion.101), channel_id=1, source_target_pairs={{4,0},{5,1},{6,2},{7,3},{8,4},{9,5},{10,6},{11,7},{12,8},{13,9},{1... | collective-permute-start | bytes 196616 | tf_op jit(solution)/shard_map/ppermute | solution.py:26
  301.9 157.4 %reduce-scatter.4.cloned.1.call-start = ((), (), s32[]{:S(2)}) async-start(), calls=%async_computation.2 | async-start | bytes 2162688
  (46 other events, 543.3 us)
Sparse Core Ops, SparseCore 0:
  302.0 155.0 all-reduce.1
Sparse Core Ops, SparseCore 1:
  308.6 112.2 reduce-scatter.3
where the time goes:
time: 470 us; the launch traced here: 468 us
  waiting for transfers between devices  315 us (67%)
  starting transfers between devices  72.7 us (15%)
  matrix products  42.4 us (9%)
  local copies, waits for them, and re-layouts  17.5 us (4%)
  between operations  16.6 us (4%)
    psum x1, waiting for transfers between devices, shards(): grad_latent = lax.psum(local_grad, 'dp')  144 us
    ppermute x15, waiting for transfers between devices, passed_along(): return lax.ppermute(block, axis, route)  117 us
    ppermute x16, waiting for transfers between devices, shifted(): return lax.ppermute(shard, axis, pairs)  54.1 us
    ppermute x16, starting transfers between devices, shifted(): return lax.ppermute(shard, axis, pairs)  40.7 us
    ppermute x15, starting transfers between devices, passed_along(): return lax.ppermute(block, axis, route)  31.9 us
  transfers between devices with their start and end apart: 33, of which 21 were waited for; matrix products, arithmetic and copies ran while one was open for 12% of the time, Pallas kernels for 0%

commit v1 on v0

v1 whole, which is shorter than its diff:
```python
import functools
import jax
import jax.numpy as jnp
from jax import lax
from jax.experimental import pallas as pl
from jax.experimental.pallas import tpu as pltpu
from jax.sharding import PartitionSpec as P

LAT = 512
ROPE = 64
NOPE = 128
ROWS = 256
HEADS_HERE = 4
WIDE = 640
SLOTS = 5
SCALE = (NOPE + ROPE) ** -0.5
LOG2E = 1.4426950408889634
LOW = -1e30
MESH = pl.DeviceIdType.MESH
F32 = jnp.float32
BF16 = jnp.bfloat16
NT = (((1,), (1,)), ((), ()))
NN = (((1,), (0,)), ((), ()))


def mm(a, b, dims=NN):
    return lax.dot_general(a, b, dims, preferred_element_type=F32)


def kernel(
    q_ref, lat_ref, go_ref, doc_ref, upk_ref, upv_ref,
    dq_ref, dlat_ref, dupk_ref, dupv_ref,
    win, qx, ups, kv, kxt, latt, probs, gprobs, stats, bias, dqt, dkv,
    part, sib_out, sib_in, ys_out, ys_own, ys_in, own_out, own_in, own_keep, gather,
    g_out, g_in, g_own, gx_out, gx_in, gz_out, gz_in,
    s_near, r_near, s_y, r_y, s_fw, r_fw, s_sib, r_sib, s_ys, r_ys,
    s_own, r_own, s_ag, r_ag, s_g, r_g, s_gx, r_gx, s_gz, r_gz,
):
    dp = lax.axis_index("dp")
    ctx = lax.axis_index("ctx")
    y, zl = lax.div(dp, 2), lax.rem(dp, 2)
    x, zh, core = lax.div(ctx, 8), lax.rem(lax.div(ctx, 2), 4), lax.rem(ctx, 2)
    sib = (dp, ctx + 1 - 2 * core)

    def at_ctx(by):
        return lax.rem(ctx + by + 32, 32)

    def at_y(by):
        return (lax.rem(y + by + 8, 8) * 2 + zl, ctx)

    def at_dp(by):
        return (lax.rem(dp + by + 16, 16), ctx)

    def at_x(by):
        return (dp, lax.rem(x + by + 4, 4) * 8 + zh * 2 + core)

    def at_zh(by):
        return (dp, x * 8 + lax.rem(zh + by + 4, 4) * 2 + core)

    def owner(by, other):
        mate = dp + 1 - 2 * zl if other else dp
        return (mate, at_ctx(by))

    barrier = pltpu.get_barrier_semaphore()
    senders = [sib, (dp, at_ctx(-2)), (dp, at_ctx(-4))]
    senders += [owner(by, other) for by in (0, 2, 4) for other in (0, 1) if by or other]
    senders += [at_dp(-i) for i in range(1, 16)]
    senders += [at_x(-i) for i in range(1, 4)]
    senders += [at_zh(-i) for i in range(1, 4)]
    for sender in senders:
        pl.semaphore_signal(barrier, inc=1, device_id=sender, device_id_type=MESH)

    def remote(src, dst, send, recv, to):
        return pltpu.make_async_remote_copy(
            src_ref=src, dst_ref=dst, send_sem=send, recv_sem=recv,
            device_id=to, device_id_type=MESH,
        )

    doc_row = doc_ref[...].astype(F32)
    line = lax.broadcasted_iota(jnp.int32, (ROWS, ROWS), 0)
    lane = lax.broadcasted_iota(jnp.int32, (ROWS, ROWS), 1)
    doc_col = jnp.sum(jnp.where(line == lane, doc_row, 0.0), axis=1, keepdims=True)
    win[4, :, :LAT] = lat_ref[:, :LAT]
    tail = jnp.concatenate([lat_ref[:, LAT:].astype(F32), jnp.zeros((ROWS, 64), F32)], axis=1)
    tail_lane = lax.broadcasted_iota(jnp.int32, (ROWS, 128), 1)
    win[4, :, LAT:] = jnp.where(tail_lane == 64, doc_col, tail).astype(BF16)

    pl.semaphore_wait(barrier, len(senders))

    def shares(slot, who):
        return win.at[slot, pl.ds(pl.multiple_of(who * 32, 32), 32), :]

    to_near = remote(shares(4, y), shares(2, y), s_near.at[0], r_near.at[0], (dp, at_ctx(2)))
    to_far = remote(shares(4, y), shares(0, y), s_near.at[1], r_near.at[1], (dp, at_ctx(4)))
    to_far.start()
    to_near.start()

    fw_own = remote(win.at[4], win.at[3], s_fw.at[0], r_fw.at[0], sib)
    fw_mid = remote(win.at[2], win.at[3], s_fw.at[0], r_fw.at[0], sib)
    fw_mid_low = remote(win.at[2], win.at[1], s_fw.at[1], r_fw.at[1], sib)
    fw_far_low = remote(win.at[0], win.at[1], s_fw.at[1], r_fw.at[1], sib)

    @pl.when(core == 0)
    def _():
        fw_own.start()

    def along_y(slot, index, by):
        return remote(
            shares(slot, y), shares(slot, y), s_y.at[index, by - 1], r_y.at[index, by - 1], at_y(by)
        )

    for h in range(HEADS_HERE):
        qx[:, h * 256 : h * 256 + 128] = q_ref[:, h * 192 : h * 192 + 128]
        qx[:, h * 256 + 128 : h * 256 + 256] = jnp.concatenate(
            [q_ref[:, h * 192 + 128 : h * 192 + 192], jnp.zeros((ROWS, 64), BF16)], axis=1
        )
    ups[:, :512] = upk_ref[...]
    ups[:, 512:] = upv_ref[...]
    dqt[...] = jnp.zeros_like(dqt)

    to_far.wait_recv()
    for by in (4, 3, 5, 2, 6, 1, 7):
        along_y(0, 1, by).start()
    to_near.wait_recv()
    for by in (4, 3, 5, 2, 6, 1, 7):
        along_y(2, 0, by).start()

    def scores(t, carry):
        slot = lax.rem(4 + 3 * t, 5)

        @pl.when(t == 1)
        def _():
            for by in range(1, 8):
                along_y(2, 0, by).wait_recv()

            @pl.when(core == 0)
            def _():
                fw_mid_low.start()

            @pl.when(core == 1)
            def _():
                fw_mid.start()

        @pl.when(t == 2)
        def _():
            for by in range(1, 8):
                along_y(0, 1, by).wait_recv()

            @pl.when(core == 1)
            def _():
                fw_far_low.start()

        @pl.when(t == 3)
        def _():
            fw_own.wait_recv()

        @pl.when(t == 4)
        def _():
            fw_mid_low.wait_recv()

        start = pl.multiple_of(slot * ROWS, ROWS)
        block = win[slot]
        latent = block[:, :LAT]
        rope = block[:, LAT:]
        for n in range(4):
            kv[pl.ds(start, ROWS), n * 256 : n * 256 + 256] = mm(
                latent, ups[:, n * 256 : n * 256 + 256]
            ).astype(BF16)
        keys = kv[pl.ds(start, ROWS), :512]
        kxt[slot, :512, :] = keys.T
        kxt[slot, 512:, :] = rope.T
        flipped = latent.T
        for g in range(32):
            row = (g % 2) * 256 + (g // 2) * 16
            latt[row : row + 16, pl.ds(start, ROWS)] = flipped[g * 16 : g * 16 + 16, :]
        docs = rope[:, 64:65].astype(F32)
        past = jnp.logical_or(slot < 4, line <= lane)
        bias[...] = jnp.where(jnp.logical_and(docs == doc_row, past), 0.0, LOW)
        for h in range(HEADS_HERE):
            cols = slice(h * 256, h * 256 + 256)
            key = kv[pl.ds(start, ROWS), h * 128 : h * 128 + 128]
            value = kv[pl.ds(start, ROWS), 512 + h * 128 : 640 + h * 128]
            s = mm(jnp.concatenate([key, rope], axis=1), qx[:, cols], NT) + bias[...]
            top = jnp.max(s, axis=0, keepdims=True)
            p = jnp.exp2((s - top) * (SCALE * LOG2E))
            gp = mm(value, go_ref[:, h * 128 : h * 128 + 128], NT)
            probs[pl.ds(start, ROWS), cols] = p
            gprobs[pl.ds(start, ROWS), cols] = gp
            stats[0, pl.ds(slot, 1), cols] = top
            stats[1, pl.ds(slot, 1), cols] = jnp.sum(p, axis=0, keepdims=True)
            stats[2, pl.ds(slot, 1), cols] = jnp.sum(p * gp, axis=0, keepdims=True)
        return carry

    lax.fori_loop(0, SLOTS, scores, 0)

    tops = stats[0, 0:SLOTS, :]
    factor = jnp.exp2((tops - jnp.max(tops, axis=0, keepdims=True)) * (SCALE * LOG2E))
    total = jnp.sum(stats[1, 0:SLOTS, :] * factor, axis=0, keepdims=True)
    delta = jnp.sum(stats[2, 0:SLOTS, :] * factor, axis=0, keepdims=True) / total
    stats[0, 0:SLOTS, :] = factor / total
    stats[1, 0:1, :] = delta

    up_low = remote(sib_out.at[0], sib_in.at[0], s_sib.at[0], r_sib.at[0], sib)
    up_high = remote(sib_out.at[1], sib_in.at[1], s_sib.at[1], r_sib.at[1], sib)

    def scatter_y(index, by):
        there = pl.multiple_of(lax.rem(y + by, 8) * 32, 32)
        return remote(
            ys_out.at[index, pl.ds(there, 32), :], ys_in.at[index, by - 1],
            s_ys.at[index, by - 1], r_ys.at[index, by - 1], at_y(by),
        )

    def grads(t, carry):
        slot = jnp.minimum(t + 1 - 2 * lax.rem(t, 2), 4)
        start = pl.multiple_of(slot * ROWS, ROWS)
        rope_sum = jnp.zeros((ROWS, 128), F32)
        for h in range(HEADS_HERE):
            cols = slice(h * 256, h * 256 + 256)
            p = probs[pl.ds(start, ROWS), cols] * stats[0, pl.ds(slot, 1), cols]
            ds = (SCALE * p * (gprobs[pl.ds(start, ROWS), cols] - stats[1, 0:1, cols])).astype(BF16)
            dv = mm(p.astype(BF16), go_ref[:, h * 128 : h * 128 + 128])
            dk = mm(ds, qx[:, cols])
            dkv[pl.ds(start, ROWS), h * 128 : h * 128 + 128] = dk[:, :128].astype(BF16)
            dkv[pl.ds(start, ROWS), 512 + h * 128 : 640 + h * 128] = dv.astype(BF16)
            rope_sum = rope_sum + dk[:, 128:]
            key_t = jnp.concatenate(
                [kxt[slot, h * 128 : h * 128 + 128, :], kxt[slot, 512:, :]], axis=0
            )
            dqt[h] += mm(key_t, ds)
        part[:, LAT:] = rope_sum
        both = dkv[pl.ds(start, ROWS), :]
        for n in range(2):
            part[:, n * 256 : n * 256 + 256] = mm(both, ups[n * 256 : n * 256 + 256, :], NT)

        def add(which):
            part[...] += sib_in[which].astype(F32)

        def leave(index):
            ys_out[index] = part[...].astype(BF16)
            ys_own[index] = part[pl.ds(pl.multiple_of(y * 32, 32), 32), :]
            for by in (4, 3, 5, 2, 6, 1, 7):
                scatter_y(index, by).start()

        @pl.when(t == 0)
        def _():
            sib_out[0] = part[...].astype(BF16)
            up_low.start()

        @pl.when(t == 1)
        def _():
            @pl.when(core == 1)
            def _():
                up_low.wait_recv()
                add(0)

            leave(0)

        @pl.when(t == 2)
        def _():
            sib_out[1] = part[...].astype(BF16)
            up_high.start()

        @pl.when(t == 3)
        def _():
            @pl.when(core == 0)
            def _():
                up_low.wait_recv()
                add(0)

            @pl.when(core == 1)
            def _():
                up_high.wait_recv()
                add(1)

            leave(1)

        @pl.when(t == 4)
        def _():
            @pl.when(core == 0)
            def _():
                up_high.wait_recv()
                add(1)

            leave(2)

        return carry

    lax.fori_loop(0, SLOTS, grads, 0)

    theirs = pl.multiple_of((1 - core) * 256, 256)
    mine = pl.multiple_of(core * 256, 256)
    to_sib = remote(g_out, g_in, s_g.at[0], r_g.at[0], sib)
    for n in range(4):
        g_out[:, n * 256 : n * 256 + 256] = mm(
            latt[pl.ds(theirs, 256), :], dkv[:, n * 256 : n * 256 + 256]
        ).astype(BF16)
    to_sib.start()
    for n in range(4):
        g_own[:, n * 256 : n * 256 + 256] = mm(
            latt[pl.ds(mine, 256), :], dkv[:, n * 256 : n * 256 + 256]
        )
    to_sib.wait_recv()
    g_own[...] += g_in[...].astype(F32)
    gx_out[...] = g_own[...].astype(BF16)

    def scatter_x(by):
        there = pl.multiple_of(lax.rem(x + by, 4) * 64, 64)
        return remote(
            gx_out.at[pl.ds(there, 64), :], gx_in.at[by - 1], s_gx.at[by - 1], r_gx.at[by - 1], at_x(by)
        )

    for by in (2, 1, 3):
        scatter_x(by).start()

    def to_owner(index, other):
        slot = index * 2 + other
        part_of = lax.rem(zl + other, 2)
        return remote(
            own_out.at[index, pl.ds(pl.multiple_of(part_of * 16, 16), 16), :], own_in.at[slot],
            s_own.at[slot], r_own.at[slot], owner(-4 + 2 * index, other),
        )

    for index in range(3):
        here = ys_own[index]
        for by in range(1, 8):
            scatter_y(index, by).wait_recv()
        for by in range(1, 8):
            here = here + ys_in[index, by - 1].astype(F32)
        own_out[index] = here.astype(BF16)
        if index == 2:
            own_keep[...] = here
        for other in (0, 1):
            if index < 2 or other:
                to_owner(index, other).start()

    for h in range(HEADS_HERE):
        dq = dqt[h].T
        dq_ref[:, h * 192 : h * 192 + 192] = dq[:, :192].astype(BF16)

    for by in range(1, 4):
        scatter_x(by).wait_recv()
    g_sum = g_own[pl.ds(pl.multiple_of(x * 64, 64), 64), :]
    for by in range(1, 4):
        g_sum = g_sum + gx_in[by - 1].astype(F32)
    g_own[0:64, :] = g_sum
    gz_out[...] = g_sum.astype(BF16)

    def scatter_zh(by):
        there = pl.multiple_of(lax.rem(zh + by, 4) * 16, 16)
        return remote(
            gz_out.at[pl.ds(there, 16), :], gz_in.at[by - 1], s_gz.at[by - 1], r_gz.at[by - 1], at_zh(by)
        )

    for by in (2, 1, 3):
        scatter_zh(by).start()

    for index in range(3):
        for other in (0, 1):
            if index < 2 or other:
                to_owner(index, other).wait_recv()
    final = own_keep[pl.ds(pl.multiple_of(zl * 16, 16), 16), :]
    for slot in range(5):
        final = final + own_in[slot if slot < 4 else 5].astype(F32)
    my_rows = pl.ds(pl.multiple_of(dp * 16, 16), 16)
    gather[my_rows, :] = final.astype(BF16)

    def to_all(by):
        return remote(
            gather.at[my_rows, :], gather.at[my_rows, :], s_ag.at[by - 1], r_ag.at[by - 1], at_dp(by)
        )

    for by in (8, 7, 9, 6, 10, 5, 11, 4, 12, 3, 13, 2, 14, 1, 15):
        to_all(by).start()

    for by in range(1, 4):
        scatter_zh(by).wait_recv()
    g_last = g_own[pl.ds(pl.multiple_of(zh * 16, 16), 16), :]
    for by in range(1, 4):
        g_last = g_last + gz_in[by - 1].astype(F32)
    dupk_ref[...] = g_last[:, :512]
    dupv_ref[...] = g_last[:, 512:]

    for by in range(1, 16):
        to_all(by).wait_recv()
    dlat_ref[...] = gather[:, : LAT + ROPE].astype(F32)

    to_near.wait_send()
    to_far.wait_send()
    fw_own.wait_send()
    fw_mid_low.wait_send()
    for by in range(1, 8):
        along_y(2, 0, by).wait_send()
        along_y(0, 1, by).wait_send()
        for index in range(3):
            scatter_y(index, by).wait_send()
    up_low.wait_send()
    up_high.wait_send()
    to_sib.wait_send()
    for by in range(1, 4):
        scatter_x(by).wait_send()
        scatter_zh(by).wait_send()
    for index in range(3):
        for other in (0, 1):
            if index < 2 or other:
                to_owner(index, other).wait_send()
    for by in range(1, 16):
        to_all(by).wait_send()


def shards(queries, latent, grad_out, doc_ids, up_key, up_value):
    vmem = pl.BlockSpec(memory_space=pltpu.VMEM)
    dma = pltpu.SemaphoreType.DMA
    return tuple(pl.pallas_call(
        kernel,
        out_shape=(
            jax.ShapeDtypeStruct((ROWS, 768), BF16),
            jax.ShapeDtypeStruct((ROWS, LAT + ROPE), F32),
            jax.ShapeDtypeStruct((16, 512), F32),
            jax.ShapeDtypeStruct((16, 512), F32),
        ),
        in_specs=[vmem] * 6,
        out_specs=(vmem,) * 4,
        scratch_shapes=[
            pltpu.VMEM((SLOTS, ROWS, WIDE), BF16),
            pltpu.VMEM((ROWS, 1024), BF16),
            pltpu.VMEM((LAT, 1024), BF16),
            pltpu.VMEM((SLOTS * ROWS, 1024), BF16),
            pltpu.VMEM((SLOTS, WIDE, ROWS), BF16),
            pltpu.VMEM((LAT, SLOTS * ROWS), BF16),
            pltpu.VMEM((SLOTS * ROWS, 1024), F32),
            pltpu.VMEM((SLOTS * ROWS, 1024), F32),
            pltpu.VMEM((3, 8, 1024), F32),
            pltpu.VMEM((ROWS, ROWS), F32),
            pltpu.VMEM((HEADS_HERE, 256, ROWS), F32),
            pltpu.VMEM((SLOTS * ROWS, 1024), BF16),
            pltpu.VMEM((ROWS, WIDE), F32),
            pltpu.VMEM((2, ROWS, WIDE), BF16),
            pltpu.VMEM((2, ROWS, WIDE), BF16),
            pltpu.VMEM((3, ROWS, WIDE), BF16),
            pltpu.VMEM((3, 32, WIDE), F32),
            pltpu.VMEM((3, 7, 32, WIDE), BF16),
            pltpu.VMEM((3, 32, WIDE), BF16),
            pltpu.VMEM((6, 16, WIDE), BF16),
            pltpu.VMEM((32, WIDE), F32),
            pltpu.VMEM((ROWS, WIDE), BF16),
            pltpu.VMEM((256, 1024), BF16),
            pltpu.VMEM((256, 1024), BF16),
            pltpu.VMEM((256, 1024), F32),
            pltpu.VMEM((256, 1024), BF16),
            pltpu.VMEM((3, 64, 1024), BF16),
            pltpu.VMEM((64, 1024), BF16),
            pltpu.VMEM((3, 16, 1024), BF16),
            dma((2,)), dma((2,)),
            dma((2, 7)), dma((2, 7)),
            dma((2,)), dma((2,)),
            dma((2,)), dma((2,)),
            dma((3, 7)), dma((3, 7)),
            dma((6,)), dma((6,)),
            dma((15,)), dma((15,)),
            dma((1,)), dma((1,)),
            dma((3,)), dma((3,)),
            dma((3,)), dma((3,)),
        ],
        compiler_params=pltpu.CompilerParams(
            collective_id=0, has_side_effects=True, vmem_limit_bytes=56 * 1024 * 1024
        ),
        name="mla_backward",
    )(queries, latent, grad_out, doc_ids.reshape(1, ROWS), up_key, up_value))


def solution(mesh):
    return jax.shard_map(
        shards,
        mesh=mesh,
        in_specs=(P("ctx", "dp"), P("ctx", None), P("ctx", "dp"), P("ctx"), P(None, "dp"), P(None, "dp")),
        out_specs=(P("ctx", "dp"), P("ctx", None), P("ctx", "dp"), P("ctx", "dp")),
        check_vma=False,
    )
```

time: 470 us -> 87.9 us (0.19)
  the two profiles are of different devices: /device:TPU:2 before, /device:TPU:1 now
where the time goes in v1:
time: 87.9 us; the launch traced here: 87.2 us
  Pallas kernels  80.4 us (91%)
  local copies, waits for them, and re-layouts  6.17 us (7%)
    pallas_call x1, Pallas kernels, shards(): pl.pallas_call(kernel, out_shape=(jax.ShapeDtypeStruct((ROWS, 768), BF16)...  80.4 us
    unnamed x10, local copies, waits for them, and re-layouts  4 us
    pallas_call x1, local copies, waits for them, and re-layouts, shards(): pl.pallas_call(kernel, out_shape=(jax.ShapeDtypeStruct((ROWS, 768), BF16)...  2.17 us

profile of v1, /device:TPU:1, one launch (start us, length us, event | category | flops | bytes accessed | tf_op | source)
XLA Modules:
  0.0 87.2 jit_solution(16332403838805204948)
XLA Ops:
  0.6 1.9 %copy.10.lat_ref = bf16[256,576]{1,0:T(8,128)(2,1)} copy(bf16[256,576]{0,1:T(8,128)(2,1)} %param.7) | data formatting | bytes 589824 | tf_op args[1]
  2.5 80.4 %mla_backward.1 = (bf16[256,768]{1,0:T(8,128)(2,1)}, f32[256,576]{1,0:T(8,128)}, f32[16,512]{1,0:T(8,128)}, f32[16,512]{1,0:T(8,128)}) custom-call(bf16[256,768]{1,0:T(8,128)(2,1)} %q_ref.1, bf16[256,576]{1,0:T(8,128)(2,1)} %copy.10.lat_ref, bf16[256,512]{1,0:T(8,128)(2,1)} %go_ref.1, s32[1,256]{1,0:T(1,128)} %bitcast.1, bf16[512,512]{1,0:T(8,128)(2,1)} %upk_ref.1, ...), custom_call_target="tpu_custom_call" | custom-call | tf_op jit(solution)/shard_map/mla_backward/pallas_call | solution.py:413
  82.9 0.0 copy-start
  82.9 2.2 %copy.11 = f32[256,576]{0,1:T(8,128)} copy(f32[256,576]{1,0:T(8,128)} %get-tuple-element.5) | data formatting | bytes 1179648 | tf_op jit(solution)/shard_map/mla_backward/pallas_call | solution.py:413
  85.1 0.0 copy-done
  85.1 0.0 copy-start.2
  85.1 0.7 copy.15
  85.8 0.0 copy-done.2
  85.8 0.0 copy-start.1
  85.8 0.6 copy.16
  86.4 0.2 copy-done.1
  86.6 0.6 copy.17
Async XLA Ops:
  82.9 2.2 %copy-start = (bf16[256,768]{1,0:T(8,128)(2,1)S(1)}, bf16[256,768]{1,0:T(8,128)(2,1)}, u32[]{:S(2)}) copy-start(bf16[256,768]{1,0:T(8,128)(2,1)} %get-tuple-element.12) | copy-start | bytes 1179652
  85.1 0.8 copy-start.2
  85.8 0.8 copy-start.1

commit v2 on v1

--- a/solution.py
+++ b/solution.py
@@ -28,12 +28,12 @@
 
 
 def kernel(
-    q_ref, lat_ref, go_ref, doc_ref, upk_ref, upv_ref,
-    dq_ref, dlat_ref, dupk_ref, dupv_ref,
-    win, qx, ups, kv, kxt, latt, probs, gprobs, stats, bias, dqt, dkv,
-    part, sib_out, sib_in, ys_out, ys_own, ys_in, own_out, own_in, own_keep, gather,
+    q_any, lat_any, go_any, doc_any, upk_any, upv_any,
+    dq_ref, dlat_ref, dup_ref,
+    q_ref, lat_ref, go_ref, doc_ref, win, qx, ups, kv, kxt, latt, probs, gprobs, stats, bias, dqt, dkv,
+    part, sib_out, sib_in, ys_out, ys_own, ys_in, own_out, own_in, own_keep,
     g_out, g_in, g_own, gx_out, gx_in, gz_out, gz_in,
-    s_near, r_near, s_y, r_y, s_fw, r_fw, s_sib, r_sib, s_ys, r_ys,
+    s_in, s_z, r_z, s_y, r_y, s_fw, r_fw, s_sib, r_sib, s_ys, r_ys,
     s_own, r_own, s_ag, r_ag, s_g, r_g, s_gx, r_gx, s_gz, r_gz,
 ):
     dp = lax.axis_index("dp")
@@ -70,18 +70,30 @@
     for sender in senders:
         pl.semaphore_signal(barrier, inc=1, device_id=sender, device_id_type=MESH)
 
+    loads = [
+        pltpu.make_async_copy(src, dst, s_in.at[i])
+        for i, (src, dst) in enumerate((
+            (lat_any, lat_ref), (doc_any, doc_ref), (upk_any, ups.at[:, :512]),
+            (upv_any, ups.at[:, 512:]), (q_any, q_ref), (go_any, go_ref),
+        ))
+    ]
+    for load in loads:
+        load.start()
+
     def remote(src, dst, send, recv, to):
         return pltpu.make_async_remote_copy(
             src_ref=src, dst_ref=dst, send_sem=send, recv_sem=recv,
             device_id=to, device_id_type=MESH,
         )
 
+    loads[0].wait()
+    loads[1].wait()
     doc_row = doc_ref[...].astype(F32)
     line = lax.broadcasted_iota(jnp.int32, (ROWS, ROWS), 0)
     lane = lax.broadcasted_iota(jnp.int32, (ROWS, ROWS), 1)
     doc_col = jnp.sum(jnp.where(line == lane, doc_row, 0.0), axis=1, keepdims=True)
-    win[4, :, :LAT] = lat_ref[:, :LAT]
-    tail = jnp.concatenate([lat_ref[:, LAT:].astype(F32), jnp.zeros((ROWS, 64), F32)], axis=1)
+    win[4, :, :LAT] = lat_ref[:LAT, :].T
+    tail = jnp.concatenate([lat_ref[LAT:, :].astype(F32), jnp.zeros((64, ROWS), F32)], axis=0).T
     tail_lane = lax.broadcasted_iota(jnp.int32, (ROWS, 128), 1)
     win[4, :, LAT:] = jnp.where(tail_lane == 64, doc_col, tail).astype(BF16)
 
@@ -90,10 +102,16 @@
     def shares(slot, who):
         return win.at[slot, pl.ds(pl.multiple_of(who * 32, 32), 32), :]
 
-    to_near = remote(shares(4, y), shares(2, y), s_near.at[0], r_near.at[0], (dp, at_ctx(2)))
-    to_far = remote(shares(4, y), shares(0, y), s_near.at[1], r_near.at[1], (dp, at_ctx(4)))
-    to_far.start()
-    to_near.start()
+    def along_z(index, half):
+        who = lax.rem(y + 4 * half, 8)
+        return remote(
+            shares(4, who), shares(2 - 2 * index, who), s_z.at[index, half], r_z.at[index, half],
+            (dp, at_ctx(2 + 2 * index)),
+        )
+
+    for index in (0, 1):
+        for half in (0, 1):
+            along_z(index, half).start()
 
     fw_own = remote(win.at[4], win.at[3], s_fw.at[0], r_fw.at[0], sib)
     fw_mid = remote(win.at[2], win.at[3], s_fw.at[0], r_fw.at[0], sib)
@@ -104,34 +122,36 @@
     def _():
         fw_own.start()
 
-    def along_y(slot, index, by):
-        return remote(
-            shares(slot, y), shares(slot, y), s_y.at[index, by - 1], r_y.at[index, by - 1], at_y(by)
-        )
+    passes = ((2, 0), (-2, 0), (1, 0), (-1, 0), (1, 4), (-1, 4))
+
+    def along_y(index, j):
+        by, more = passes[j]
+        rows = shares(2 - 2 * index, lax.rem(y + more, 8))
+        return remote(rows, rows, s_y.at[index, j], r_y.at[index, j], at_y(by))
+
+    for load in loads[2:]:
+        load.wait()
 
     for h in range(HEADS_HERE):
         qx[:, h * 256 : h * 256 + 128] = q_ref[:, h * 192 : h * 192 + 128]
         qx[:, h * 256 + 128 : h * 256 + 256] = jnp.concatenate(
             [q_ref[:, h * 192 + 128 : h * 192 + 192], jnp.zeros((ROWS, 64), BF16)], axis=1
         )
-    ups[:, :512] = upk_ref[...]
-    ups[:, 512:] = upv_ref[...]
     dqt[...] = jnp.zeros_like(dqt)
 
-    to_far.wait_recv()
-    for by in (4, 3, 5, 2, 6, 1, 7):
-        along_y(0, 1, by).start()
-    to_near.wait_recv()
-    for by in (4, 3, 5, 2, 6, 1, 7):
-        along_y(2, 0, by).start()
+    for index in (0, 1):
+        for half in (0, 1):
+            along_z(index, half).wait_recv()
+        for j in range(6):
+            along_y(index, j).start()
 
     def scores(t, carry):
         slot = lax.rem(4 + 3 * t, 5)
 
         @pl.when(t == 1)
         def _():
-            for by in range(1, 8):
-                along_y(2, 0, by).wait_recv()
+            for j in range(6):
+                along_y(0, j).wait_recv()
 
             @pl.when(core == 0)
             def _():
@@ -143,8 +163,8 @@
 
         @pl.when(t == 2)
         def _():
-            for by in range(1, 8):
-                along_y(0, 1, by).wait_recv()
+            for j in range(6):
+                along_y(1, j).wait_recv()
 
             @pl.when(core == 1)
             def _():
@@ -203,12 +223,32 @@
     up_low = remote(sib_out.at[0], sib_in.at[0], s_sib.at[0], r_sib.at[0], sib)
     up_high = remote(sib_out.at[1], sib_in.at[1], s_sib.at[1], r_sib.at[1], sib)
 
-    def scatter_y(index, by):
-        there = pl.multiple_of(lax.rem(y + by, 8) * 32, 32)
+    def share_of(by):
+        return pl.multiple_of(lax.rem(y + by + 8, 8) * 32, 32)
+
+    def hop(index, step, way):
+        lane_of = 0 if way > 0 else 1
+        rows = pl.ds(share_of(way * (5 - step)), 32)
+        into = pl.ds(0, 32)
+        if step == 1:
+            rows = pl.ds(pl.multiple_of(share_of(4) + 16 * lane_of, 16), 16)
+            into = pl.ds(0, 16)
         return remote(
-            ys_out.at[index, pl.ds(there, 32), :], ys_in.at[index, by - 1],
-            s_ys.at[index, by - 1], r_ys.at[index, by - 1], at_y(by),
-        )
+            ys_out.at[index, rows, :], ys_in.at[index, lane_of, step - 1, into, :],
+            s_ys.at[index, lane_of, step - 1], r_ys.at[index, lane_of, step - 1], at_y(way),
+        )
+
+    def relay(index, step):
+        for way in (1, -1):
+            lane_of = 0 if way > 0 else 1
+            hop(index, step - 1, way).wait_recv()
+            first, count = share_of(way * (5 - step)), 32
+            if step == 2:
+                first, count = pl.multiple_of(first + 16 * lane_of, 16), 16
+            rows = pl.ds(first, count)
+            came = ys_in[index, lane_of, step - 2, 0:count, :].astype(F32)
+            ys_out[index, rows, :] = (ys_out[index, rows, :].astype(F32) + came).astype(BF16)
+            hop(index, step, way).start()
 
     def grads(t, carry):
         slot = jnp.minimum(t + 1 - 2 * lax.rem(t, 2), 4)
@@ -238,8 +278,8 @@
         def leave(index):
             ys_out[index] = part[...].astype(BF16)
             ys_own[index] = part[pl.ds(pl.multiple_of(y * 32, 32), 32), :]
-            for by in (4, 3, 5, 2, 6, 1, 7):
-                scatter_y(index, by).start()
+            hop(index, 1, 1).start()
+            hop(index, 1, -1).start()
 
         @pl.when(t == 0)
         def _():
@@ -272,6 +312,7 @@
                 up_high.wait_recv()
                 add(1)
 
+            relay(0, 2)
             leave(1)
 
         @pl.when(t == 4)
@@ -295,10 +336,15 @@
             latt[pl.ds(theirs, 256), :], dkv[:, n * 256 : n * 256 + 256]
         ).astype(BF16)
     to_sib.start()
+    relay(0, 3)
+    relay(1, 2)
     for n in range(4):
         g_own[:, n * 256 : n * 256 + 256] = mm(
             latt[pl.ds(mine, 256), :], dkv[:, n * 256 : n * 256 + 256]
         )
+    relay(2, 2)
+    relay(0, 4)
+    relay(1, 3)
     to_sib.wait_recv()
     g_own[...] += g_in[...].astype(F32)
     gx_out[...] = g_own[...].astype(BF16)
@@ -320,12 +366,11 @@
             s_own.at[slot], r_own.at[slot], owner(-4 + 2 * index, other),
         )
 
-    for index in range(3):
+    def settle(index):
         here = ys_own[index]
-        for by in range(1, 8):
-            scatter_y(index, by).wait_recv()
-        for by in range(1, 8):
-            here = here + ys_in[index, by - 1].astype(F32)
+        for way in (1, -1):
+            hop(index, 4, way).wait_recv()
+            here = here + ys_in[index, 0 if way > 0 else 1, 3].astype(F32)
         own_out[index] = here.astype(BF16)
         if index == 2:
             own_keep[...] = here
@@ -333,9 +378,17 @@
             if index < 2 or other:
                 to_owner(index, other).start()
 
+    relay(2, 3)
+    settle(0)
+    relay(1, 4)
+
     for h in range(HEADS_HERE):
         dq = dqt[h].T
         dq_ref[:, h * 192 : h * 192 + 192] = dq[:, :192].astype(BF16)
+
+    relay(2, 4)
+    settle(1)
+    settle(2)
 
     for by in range(1, 4):
         scatter_x(by).wait_recv()
@@ -362,11 +415,11 @@
     for slot in range(5):
         final = final + own_in[slot if slot < 4 else 5].astype(F32)
     my_rows = pl.ds(pl.multiple_of(dp * 16, 16), 16)
-    gather[my_rows, :] = final.astype(BF16)
+    dlat_ref[my_rows, :] = final.astype(BF16)
 
     def to_all(by):
         return remote(
-            gather.at[my_rows, :], gather.at[my_rows, :], s_ag.at[by - 1], r_ag.at[by - 1], at_dp(by)
+            dlat_ref.at[my_rows, :], dlat_ref.at[my_rows, :], s_ag.at[by - 1], r_ag.at[by - 1], at_dp(by)
         )
 
     for by in (8, 7, 9, 6, 10, 5, 11, 4, 12, 3, 13, 2, 14, 1, 15):
@@ -377,22 +430,22 @@
     g_last = g_own[pl.ds(pl.multiple_of(zh * 16, 16), 16), :]
     for by in range(1, 4):
         g_last = g_last + gz_in[by - 1].astype(F32)
-    dupk_ref[...] = g_last[:, :512]
-    dupv_ref[...] = g_last[:, 512:]
+    dup_ref[...] = g_last
 
     for by in range(1, 16):
         to_all(by).wait_recv()
-    dlat_ref[...] = gather[:, : LAT + ROPE].astype(F32)
-
-    to_near.wait_send()
-    to_far.wait_send()
+
+    for index in (0, 1):
+        for half in (0, 1):
+            along_z(index, half).wait_send()
+        for j in range(6):
+            along_y(index, j).wait_send()
     fw_own.wait_send()
     fw_mid_low.wait_send()
-    for by in range(1, 8):
-        along_y(2, 0, by).wait_send()
-        along_y(0, 1, by).wait_send()
-        for index in range(3):
-            scatter_y(index, by).wait_send()
+    for index in range(3):
+        for step in range(1, 5):
+            for way in (1, -1):
+                hop(index, step, way).wait_send()
     up_low.wait_send()
     up_high.wait_send()
     to_sib.wait_send()
@@ -407,20 +460,27 @@
         to_all(by).wait_send()
 
 
+def write_out(dq_in, dlat_in, dup_in, dq_ref, dlat_ref, dupk_ref, dupv_ref):
+    dq_ref[...] = dq_in[...]
+    dlat_ref[...] = dlat_in[...].astype(F32).T[: LAT + ROPE, :]
+    dupk_ref[...] = dup_in[:, :512]
+    dupv_ref[...] = dup_in[:, 512:]
+
+
 def shards(queries, latent, grad_out, doc_ids, up_key, up_value):
     vmem = pl.BlockSpec(memory_space=pltpu.VMEM)
     dma = pltpu.SemaphoreType.DMA
-    return tuple(pl.pallas_call(
+    shape = jax.ShapeDtypeStruct
+    made = pl.pallas_call(
         kernel,
-        out_shape=(
-            jax.ShapeDtypeStruct((ROWS, 768), BF16),
-            jax.ShapeDtypeStruct((ROWS, LAT + ROPE), F32),
-            jax.ShapeDtypeStruct((16, 512), F32),
-            jax.ShapeDtypeStruct((16, 512), F32),
-        ),
-        in_specs=[vmem] * 6,
-        out_specs=(vmem,) * 4,
+        out_shape=(shape((ROWS, 768), BF16), shape((ROWS, WIDE), BF16), shape((16, 1024), F32)),
+        in_specs=[pl.BlockSpec(memory_space=pl.ANY)] * 6,
+        out_specs=(vmem,) * 3,
         scratch_shapes=[
+            pltpu.VMEM((ROWS, 768), BF16),
+            pltpu.VMEM((LAT + ROPE, ROWS), BF16),
+            pltpu.VMEM((ROWS, 512), BF16),
+            pltpu.VMEM((1, ROWS), jnp.int32),
             pltpu.VMEM((SLOTS, ROWS, WIDE), BF16),
             pltpu.VMEM((ROWS, 1024), BF16),
             pltpu.VMEM((LAT, 1024), BF16),
@@ -438,11 +498,10 @@
             pltpu.VMEM((2, ROWS, WIDE), BF16),
             pltpu.VMEM((3, ROWS, WIDE), BF16),
             pltpu.VMEM((3, 32, WIDE), F32),
-            pltpu.VMEM((3, 7, 32, WIDE), BF16),
+            pltpu.VMEM((3, 2, 4, 32, WIDE), BF16),
             pltpu.VMEM((3, 32, WIDE), BF16),
             pltpu.VMEM((6, 16, WIDE), BF16),
             pltpu.VMEM((32, WIDE), F32),
-            pltpu.VMEM((ROWS, WIDE), BF16),
             pltpu.VMEM((256, 1024), BF16),
             pltpu.VMEM((256, 1024), BF16),
             pltpu.VMEM((256, 1024), F32),
@@ -450,11 +509,12 @@
             pltpu.VMEM((3, 64, 1024), BF16),
             pltpu.VMEM((64, 1024), BF16),
             pltpu.VMEM((3, 16, 1024), BF16),
-            dma((2,)), dma((2,)),
-            dma((2, 7)), dma((2, 7)),
+            dma((6,)),
+            dma((2, 2)), dma((2, 2)),
+            dma((2, 6)), dma((2, 6)),
             dma((2,)), dma((2,)),
             dma((2,)), dma((2,)),
-            dma((3, 7)), dma((3, 7)),
+            dma((3, 2, 4)), dma((3, 2, 4)),
             dma((6,)), dma((6,)),
             dma((15,)), dma((15,)),
             dma((1,)), dma((1,)),
@@ -465,7 +525,19 @@
             collective_id=0, has_side_effects=True, vmem_limit_bytes=56 * 1024 * 1024
         ),
         name="mla_backward",
-    )(queries, latent, grad_out, doc_ids.reshape(1, ROWS), up_key, up_value))
+    )(queries, latent.T, grad_out, doc_ids.reshape(1, ROWS), up_key, up_value)
+    grad_queries, grad_latent, grad_up_key, grad_up_value = pl.pallas_call(
+        write_out,
+        out_shape=(
+            shape((ROWS, 768), BF16), shape((LAT + ROPE, ROWS), F32),
+            shape((16, 512), F32), shape((16, 512), F32),
+        ),
+        in_specs=[vmem] * 3,
+        out_specs=(vmem,) * 4,
+        compiler_params=pltpu.CompilerParams(vmem_limit_bytes=16 * 1024 * 1024),
+        name="write_out",
+    )(*made)
+    return grad_queries, grad_latent.T, grad_up_key, grad_up_value
 
 
 def solution(mesh):

time: 87.9 us -> 72.8 us (0.83)
  the two profiles are of different devices: /device:TPU:1 before, /device:TPU:2 now
where the time goes in v2:
time: 72.8 us; the launch traced here: 72.5 us
  Pallas kernels  69.1 us (95%)
  local copies, waits for them, and re-layouts  2.8 us (4%)
    pallas_call x1, Pallas kernels, shards(): pl.pallas_call(kernel, out_shape=(shape((ROWS, 768), BF16), shape((ROWS,...  68 us
    unnamed x6, local copies, waits for them, and re-layouts  2.8 us

profile of v2, /device:TPU:2, one launch (start us, length us, event | category | flops | bytes accessed | tf_op | source)
XLA Modules:
  0.0 72.5 jit_solution(2597895650214686313)
XLA Ops:
  0.6 68.0 %mla_backward.1 = (bf16[256,768]{1,0:T(8,128)(2,1)}, bf16[256,640]{1,0:T(8,128)(2,1)}, f32[16,1024]{1,0:T(8,128)}) custom-call(bf16[256,768]{1,0:T(8,128)(2,1)} %q_any.1, bf16[576,256]{1,0:T(8,128)(2,1)} %bitcast.3, bf16[256,512]{1,0:T(8,128)(2,1)} %go_any.1, s32[1,256]{1,0:T(1,128)} %bitcast.4, bf16[512,512]{1,0:T(8,128)(2,1)} %upk_any.1, ...), custom_call_target="tpu_custom_call" | custom-call | tf_op jit(solution)/shard_map/mla_backward/pallas_call | solution.py:474
  68.7 0.0 copy-start
  68.7 1.0 %copy-done = bf16[256,768]{1,0:T(8,128)(2,1)S(1)} copy-done((bf16[256,768]{1,0:T(8,128)(2,1)S(1)}, bf16[256,768]{1,0:T(8,128)(2,1)}, u32[]{:S(2)}) %copy-start) | copy-done | bytes 393240
  69.7 0.0 copy-start.1
  69.7 1.0 %copy-done.1 = bf16[256,640]{1,0:T(8,128)(2,1)S(1)} copy-done((bf16[256,640]{1,0:T(8,128)(2,1)S(1)}, bf16[256,640]{1,0:T(8,128)(2,1)}, u32[]{:S(2)}) %copy-start.1) | copy-done | bytes 327704
  70.6 0.0 copy-start.2
  70.6 0.8 %copy-done.2 = f32[16,1024]{1,0:T(8,128)S(1)} copy-done((f32[16,1024]{1,0:T(8,128)S(1)}, f32[16,1024]{1,0:T(8,128)}, u32[]{:S(2)}) %copy-start.2) | copy-done | bytes 65560
  71.5 1.1 %write_out.1 = (bf16[256,768]{1,0:T(8,128)(2,1)}, f32[576,256]{1,0:T(8,128)}, f32[16,512]{1,0:T(8,128)}, f32[16,512]{1,0:T(8,128)}) custom-call(bf16[256,768]{1,0:T(8,128)(2,1)S(1)} %copy-done, bf16[256,640]{1,0:T(8,128)(2,1)S(1)} %copy-done.1, f32[16,1024]{1,0:T(8,128)S(1)} %copy-done.2), custom_call_target="tpu_custom_call" | custom-call | tf_op jit(solution)/shard_map/write_out/pallas_call | solution.py:529
Async XLA Ops:
  68.7 1.0 %copy-start = (bf16[256,768]{1,0:T(8,128)(2,1)S(1)}, bf16[256,768]{1,0:T(8,128)(2,1)}, u32[]{:S(2)}) copy-start(bf16[256,768]{1,0:T(8,128)(2,1)} %get-tuple-element.11.dq_in) | copy-start | bytes 1179652
  69.7 1.0 %copy-start.1 = (bf16[256,640]{1,0:T(8,128)(2,1)S(1)}, bf16[256,640]{1,0:T(8,128)(2,1)}, u32[]{:S(2)}) copy-start(bf16[256,640]{1,0:T(8,128)(2,1)} %get-tuple-element.12.dlat_in) | copy-start | bytes 983044
  70.6 0.8 %copy-start.2 = (f32[16,1024]{1,0:T(8,128)S(1)}, f32[16,1024]{1,0:T(8,128)}, u32[]{:S(2)}) copy-start(f32[16,1024]{1,0:T(8,128)} %get-tuple-element.13.dup_in) | copy-start | bytes 196612

commit v3 on v2

--- a/solution.py
+++ b/solution.py
@@ -29,11 +29,11 @@
 
 def kernel(
     q_any, lat_any, go_any, doc_any, upk_any, upv_any,
-    dq_ref, dlat_ref, dup_ref,
-    q_ref, lat_ref, go_ref, doc_ref, win, qx, ups, kv, kxt, latt, probs, gprobs, stats, bias, dqt, dkv,
+    dq_any, dlat_any, dup_any,
+    dq_ref, dlat_ref, dup_ref, q_ref, lat_ref, go_ref, doc_ref, win, qx, ups, kv, kxt, latt, probs, gprobs, stats, bias, dqt, dkv,
     part, sib_out, sib_in, ys_out, ys_own, ys_in, own_out, own_in, own_keep,
     g_out, g_in, g_own, gx_out, gx_in, gz_out, gz_in,
-    s_in, s_z, r_z, s_y, r_y, s_fw, r_fw, s_sib, r_sib, s_ys, r_ys,
+    s_in, s_out, s_z, r_z, s_y, r_y, s_fw, r_fw, s_sib, r_sib, s_ys, r_ys,
     s_own, r_own, s_ag, r_ag, s_g, r_g, s_gx, r_gx, s_gz, r_gz,
 ):
     dp = lax.axis_index("dp")
@@ -226,32 +226,35 @@
     def share_of(by):
         return pl.multiple_of(lax.rem(y + by + 8, 8) * 32, 32)
 
-    def hop(index, step, way):
-        lane_of = 0 if way > 0 else 1
-        rows = pl.ds(share_of(way * (5 - step)), 32)
-        into = pl.ds(0, 32)
-        if step == 1:
-            rows = pl.ds(pl.multiple_of(share_of(4) + 16 * lane_of, 16), 16)
+    def hop(index, kind, way):
+        side = 0 if way > 0 else 1
+        by, dest = ((1, 1), (1, 3), (2, 4), (2, 2))[kind]
+        rows, into = pl.ds(share_of(way * dest), 32), pl.ds(0, 32)
+        if kind == 2:
+            rows = pl.ds(pl.multiple_of(share_of(4) + 16 * side, 16), 16)
             into = pl.ds(0, 16)
         return remote(
-            ys_out.at[index, rows, :], ys_in.at[index, lane_of, step - 1, into, :],
-            s_ys.at[index, lane_of, step - 1], r_ys.at[index, lane_of, step - 1], at_y(way),
-        )
-
-    def relay(index, step):
+            ys_out.at[index, rows, :], ys_in.at[index, side, kind, into, :],
+            s_ys.at[index, side, kind], r_ys.at[index, side, kind], at_y(way * by),
+        )
+
+    def relay(index):
         for way in (1, -1):
-            lane_of = 0 if way > 0 else 1
-            hop(index, step - 1, way).wait_recv()
-            first, count = share_of(way * (5 - step)), 32
-            if step == 2:
-                first, count = pl.multiple_of(first + 16 * lane_of, 16), 16
-            rows = pl.ds(first, count)
-            came = ys_in[index, lane_of, step - 2, 0:count, :].astype(F32)
-            ys_out[index, rows, :] = (ys_out[index, rows, :].astype(F32) + came).astype(BF16)
-            hop(index, step, way).start()
+            side = 0 if way > 0 else 1
+            hop(index, 1, way).wait_recv()
+            hop(index, 2, way).wait_recv()
+            rows = pl.ds(share_of(2 * way), 32)
+            more = ys_in[index, side, 1].astype(F32)
+            half = ys_in[index, side, 2, 0:16, :].astype(F32)
+            empty = jnp.zeros_like(half)
+            more = more + jnp.concatenate([empty, half] if side else [half, empty], axis=0)
+            ys_out[index, rows, :] = (ys_out[index, rows, :].astype(F32) + more).astype(BF16)
+            hop(index, 3, way).start()
 
     def grads(t, carry):
-        slot = jnp.minimum(t + 1 - 2 * lax.rem(t, 2), 4)
+        slot = jnp.where(
+            t == 0, 4 * core, jnp.where(t < 3, 2 * t - 1, jnp.where(t == 3, 2 - 2 * core, 4 - 2 * core))
+        )
         start = pl.multiple_of(slot * ROWS, ROWS)
         rope_sum = jnp.zeros((ROWS, 128), F32)
         for h in range(HEADS_HERE):
@@ -278,23 +281,19 @@
         def leave(index):
             ys_out[index] = part[...].astype(BF16)
             ys_own[index] = part[pl.ds(pl.multiple_of(y * 32, 32), 32), :]
-            hop(index, 1, 1).start()
-            hop(index, 1, -1).start()
+            for kind in (2, 1, 0):
+                for way in (1, -1):
+                    hop(index, kind, way).start()
 
         @pl.when(t == 0)
+        def _():
+            leave(0)
+
+        @pl.when(t == 1)
         def _():
             sib_out[0] = part[...].astype(BF16)
             up_low.start()
 
-        @pl.when(t == 1)
-        def _():
-            @pl.when(core == 1)
-            def _():
-                up_low.wait_recv()
-                add(0)
-
-            leave(0)
-
         @pl.when(t == 2)
         def _():
             sib_out[1] = part[...].astype(BF16)
@@ -302,26 +301,15 @@
 
         @pl.when(t == 3)
         def _():
-            @pl.when(core == 0)
-            def _():
-                up_low.wait_recv()
-                add(0)
-
-            @pl.when(core == 1)
-            def _():
-                up_high.wait_recv()
-                add(1)
-
-            relay(0, 2)
+            up_low.wait_recv()
+            add(0)
             leave(1)
+            relay(0)
 
         @pl.when(t == 4)
         def _():
-            @pl.when(core == 0)
-            def _():
-                up_high.wait_recv()
-                add(1)
-
+            up_high.wait_recv()
+            add(1)
             leave(2)
 
         return carry
@@ -336,15 +324,18 @@
             latt[pl.ds(theirs, 256), :], dkv[:, n * 256 : n * 256 + 256]
         ).astype(BF16)
     to_sib.start()
-    relay(0, 3)
-    relay(1, 2)
     for n in range(4):
         g_own[:, n * 256 : n * 256 + 256] = mm(
             latt[pl.ds(mine, 256), :], dkv[:, n * 256 : n * 256 + 256]
         )
-    relay(2, 2)
-    relay(0, 4)
-    relay(1, 3)
+    relay(1)
+
+    for h in range(HEADS_HERE):
+        dq = dqt[h].T
+        dq_ref[:, h * 192 : h * 192 + 192] = dq[:, :192].astype(BF16)
+    dq_out = pltpu.make_async_copy(dq_ref, dq_any, s_out.at[0])
+    dq_out.start()
+
     to_sib.wait_recv()
     g_own[...] += g_in[...].astype(F32)
     gx_out[...] = g_own[...].astype(BF16)
@@ -357,6 +348,7 @@
 
     for by in (2, 1, 3):
         scatter_x(by).start()
+    relay(2)
 
     def to_owner(index, other):
         slot = index * 2 + other
@@ -367,28 +359,26 @@
         )
 
     def settle(index):
+        which = lax.rem(index + 2 * core, 3)
         here = ys_own[index]
         for way in (1, -1):
-            hop(index, 4, way).wait_recv()
-            here = here + ys_in[index, 0 if way > 0 else 1, 3].astype(F32)
-        own_out[index] = here.astype(BF16)
-        if index == 2:
+            for kind in (0, 3):
+                hop(index, kind, way).wait_recv()
+                here = here + ys_in[index, 0 if way > 0 else 1, kind].astype(F32)
+        own_out[which] = here.astype(BF16)
+
+        @pl.when(which == 2)
+        def _():
             own_keep[...] = here
-        for other in (0, 1):
-            if index < 2 or other:
-                to_owner(index, other).start()
-
-    relay(2, 3)
-    settle(0)
-    relay(1, 4)
-
-    for h in range(HEADS_HERE):
-        dq = dqt[h].T
-        dq_ref[:, h * 192 : h * 192 + 192] = dq[:, :192].astype(BF16)
-
-    relay(2, 4)
-    settle(1)
-    settle(2)
+
+        @pl.when(which < 2)
+        def _():
+            to_owner(which, 0).start()
+
+        to_owner(which, 1).start()
+
+    for index in range(3):
+        settle(index)
 
     for by in range(1, 4):
         scatter_x(by).wait_recv()
@@ -431,9 +421,13 @@
     for by in range(1, 4):
         g_last = g_last + gz_in[by - 1].astype(F32)
     dup_ref[...] = g_last
+    dup_out = pltpu.make_async_copy(dup_ref, dup_any, s_out.at[1])
+    dup_out.start()
 
     for by in range(1, 16):
         to_all(by).wait_recv()
+    dlat_out = pltpu.make_async_copy(dlat_ref, dlat_any, s_out.at[2])
+    dlat_out.start()
 
     for index in (0, 1):
         for half in (0, 1):
@@ -443,9 +437,9 @@
     fw_own.wait_send()
     fw_mid_low.wait_send()
     for index in range(3):
-        for step in range(1, 5):
+        for kind in range(4):
             for way in (1, -1):
-                hop(index, step, way).wait_send()
+                hop(index, kind, way).wait_send()
     up_low.wait_send()
     up_high.wait_send()
     to_sib.wait_send()
@@ -458,25 +452,40 @@
                 to_owner(index, other).wait_send()
     for by in range(1, 16):
         to_all(by).wait_send()
-
-
-def write_out(dq_in, dlat_in, dup_in, dq_ref, dlat_ref, dupk_ref, dupv_ref):
-    dq_ref[...] = dq_in[...]
-    dlat_ref[...] = dlat_in[...].astype(F32).T[: LAT + ROPE, :]
-    dupk_ref[...] = dup_in[:, :512]
-    dupv_ref[...] = dup_in[:, 512:]
+    dq_out.wait()
+    dup_out.wait()
+    dlat_out.wait()
+
+
+def write_out(dq_in, dlat_in, dup_in, dq_any, dlat_ref, dupk_ref, dupv_ref, dlat, dup, sem):
+    copies = [
+        pltpu.make_async_copy(src, dst, sem.at[i])
+        for i, (src, dst) in enumerate(((dlat_in, dlat), (dup_in, dup), (dq_in, dq_any)))
+    ]
+    for copy in copies:
+        copy.start()
+    copies[0].wait()
+    dlat_ref[...] = dlat[...].astype(F32).T[: LAT + ROPE, :]
+    copies[1].wait()
+    dupk_ref[...] = dup[:, :512]
+    dupv_ref[...] = dup[:, 512:]
+    copies[2].wait()
 
 
 def shards(queries, latent, grad_out, doc_ids, up_key, up_value):
     vmem = pl.BlockSpec(memory_space=pltpu.VMEM)
+    anywhere = pl.BlockSpec(memory_space=pl.ANY)
     dma = pltpu.SemaphoreType.DMA
     shape = jax.ShapeDtypeStruct
     made = pl.pallas_call(
         kernel,
         out_shape=(shape((ROWS, 768), BF16), shape((ROWS, WIDE), BF16), shape((16, 1024), F32)),
-        in_specs=[pl.BlockSpec(memory_space=pl.ANY)] * 6,
-        out_specs=(vmem,) * 3,
+        in_specs=[anywhere] * 6,
+        out_specs=(anywhere,) * 3,
         scratch_shapes=[
+            pltpu.VMEM((ROWS, 768), BF16),
+            pltpu.VMEM((ROWS, WIDE), BF16),
+            pltpu.VMEM((16, 1024), F32),
             pltpu.VMEM((ROWS, 768), BF16),
             pltpu.VMEM((LAT + ROPE, ROWS), BF16),
             pltpu.VMEM((ROWS, 512), BF16),
@@ -510,6 +519,7 @@
             pltpu.VMEM((64, 1024), BF16),
             pltpu.VMEM((3, 16, 1024), BF16),
             dma((6,)),
+            dma((3,)),
             dma((2, 2)), dma((2, 2)),
             dma((2, 6)), dma((2, 6)),
             dma((2,)), dma((2,)),
@@ -532,9 +542,10 @@
             shape((ROWS, 768), BF16), shape((LAT + ROPE, ROWS), F32),
             shape((16, 512), F32), shape((16, 512), F32),
         ),
-        in_specs=[vmem] * 3,
-        out_specs=(vmem,) * 4,
-        compiler_params=pltpu.CompilerParams(vmem_limit_bytes=16 * 1024 * 1024),
+        in_specs=[anywhere] * 3,
+        out_specs=(anywhere, vmem, vmem, vmem),
+        scratch_shapes=[pltpu.VMEM((ROWS, WIDE), BF16), pltpu.VMEM((16, 1024), F32), dma((3,))],
+        compiler_params=pltpu.CompilerParams(vmem_limit_bytes=63 * 1024 * 1024),
         name="write_out",
     )(*made)
     return grad_queries, grad_latent.T, grad_up_key, grad_up_value

time: 72.8 us -> 81 us (1.11)
  the two profiles are of different devices: /device:TPU:2 before, /device:TPU:1 now
where the time goes in v3:
time: 81 us; the launch traced here: 80.8 us
  Pallas kernels  80.2 us (99%)
    pallas_call x1, Pallas kernels, shards(): pl.pallas_call(kernel, out_shape=(shape((ROWS, 768), BF16), shape((ROWS,...  66.3 us
    pallas_call x1, Pallas kernels, shards(): pl.pallas_call(write_out, out_shape=(shape((ROWS, 768), BF16), shape((LAT...  13.9 us

profile of v3, /device:TPU:1, one launch (start us, length us, event | category | flops | bytes accessed | tf_op | source)
XLA Modules:
  0.0 80.8 jit_solution(13688605874536009041)
XLA Ops:
  0.6 66.3 %mla_backward.1 = (bf16[256,768]{1,0:T(8,128)(2,1)}, bf16[256,640]{1,0:T(8,128)(2,1)}, f32[16,1024]{1,0:T(8,128)}) custom-call(bf16[256,768]{1,0:T(8,128)(2,1)} %q_any.1, bf16[576,256]{1,0:T(8,128)(2,1)} %bitcast.3, bf16[256,512]{1,0:T(8,128)(2,1)} %go_any.1, s32[1,256]{1,0:T(1,128)} %bitcast.4, bf16[512,512]{1,0:T(8,128)(2,1)} %upk_any.1, ...), custom_call_target="tpu_custom_call" | custom-call | tf_op jit(solution)/shard_map/mla_backward/pallas_call | solution.py:480
  67.0 13.9 %write_out.1 = (bf16[256,768]{1,0:T(8,128)(2,1)}, f32[576,256]{1,0:T(8,128)}, f32[16,512]{1,0:T(8,128)}, f32[16,512]{1,0:T(8,128)}) custom-call(bf16[256,768]{1,0:T(8,128)(2,1)} %get-tuple-element.11.dq_in, bf16[256,640]{1,0:T(8,128)(2,1)} %get-tuple-element.12.dlat_in, f32[16,1024]{1,0:T(8,128)} %get-tuple-element.13.dup_in), custom_call_target="tpu_custom_call" | custom-call | tf_op jit(solution)/shard_map/write_out/pallas_call | solution.py:539

commit v4 on v3

--- a/solution.py
+++ b/solution.py
@@ -146,9 +146,12 @@
             along_y(index, j).start()
 
     def scores(t, carry):
-        slot = lax.rem(4 + 3 * t, 5)
-
-        @pl.when(t == 1)
+        slot = jnp.where(
+            t == 0, 4,
+            jnp.where(t == 1, 2 + core, jnp.where(t == 2, 3 - core, jnp.where(t == 3, 0, 1))),
+        )
+
+        @pl.when(t == 1 + core)
         def _():
             for j in range(6):
                 along_y(0, j).wait_recv()
@@ -161,7 +164,7 @@
             def _():
                 fw_mid.start()
 
-        @pl.when(t == 2)
+        @pl.when(t == 3)
         def _():
             for j in range(6):
                 along_y(1, j).wait_recv()
@@ -170,7 +173,7 @@
             def _():
                 fw_far_low.start()
 
-        @pl.when(t == 3)
+        @pl.when(t == 2 - core)
         def _():
             fw_own.wait_recv()
 
@@ -329,6 +332,7 @@
             latt[pl.ds(mine, 256), :], dkv[:, n * 256 : n * 256 + 256]
         )
     relay(1)
+    relay(2)
 
     for h in range(HEADS_HERE):
         dq = dqt[h].T
@@ -348,7 +352,6 @@
 
     for by in (2, 1, 3):
         scatter_x(by).start()
-    relay(2)
 
     def to_owner(index, other):
         slot = index * 2 + other
@@ -379,23 +382,6 @@
 
     for index in range(3):
         settle(index)
-
-    for by in range(1, 4):
-        scatter_x(by).wait_recv()
-    g_sum = g_own[pl.ds(pl.multiple_of(x * 64, 64), 64), :]
-    for by in range(1, 4):
-        g_sum = g_sum + gx_in[by - 1].astype(F32)
-    g_own[0:64, :] = g_sum
-    gz_out[...] = g_sum.astype(BF16)
-
-    def scatter_zh(by):
-        there = pl.multiple_of(lax.rem(zh + by, 4) * 16, 16)
-        return remote(
-            gz_out.at[pl.ds(there, 16), :], gz_in.at[by - 1], s_gz.at[by - 1], r_gz.at[by - 1], at_zh(by)
-        )
-
-    for by in (2, 1, 3):
-        scatter_zh(by).start()
 
     for index in range(3):
         for other in (0, 1):
@@ -414,6 +400,23 @@
 
     for by in (8, 7, 9, 6, 10, 5, 11, 4, 12, 3, 13, 2, 14, 1, 15):
         to_all(by).start()
+
+    for by in range(1, 4):
+        scatter_x(by).wait_recv()
+    g_sum = g_own[pl.ds(pl.multiple_of(x * 64, 64), 64), :]
+    for by in range(1, 4):
+        g_sum = g_sum + gx_in[by - 1].astype(F32)
+    g_own[0:64, :] = g_sum
+    gz_out[...] = g_sum.astype(BF16)
+
+    def scatter_zh(by):
+        there = pl.multiple_of(lax.rem(zh + by, 4) * 16, 16)
+        return remote(
+            gz_out.at[pl.ds(there, 16), :], gz_in.at[by - 1], s_gz.at[by - 1], r_gz.at[by - 1], at_zh(by)
+        )
+
+    for by in (2, 1, 3):
+        scatter_zh(by).start()
 
     for by in range(1, 4):
         scatter_zh(by).wait_recv()
@@ -457,10 +460,10 @@
     dlat_out.wait()
 
 
-def write_out(dq_in, dlat_in, dup_in, dq_any, dlat_ref, dupk_ref, dupv_ref, dlat, dup, sem):
+def write_out(dq_in, dlat_in, dup_in, dq_ref, dlat_ref, dupk_ref, dupv_ref, dlat, dup, sem):
     copies = [
         pltpu.make_async_copy(src, dst, sem.at[i])
-        for i, (src, dst) in enumerate(((dlat_in, dlat), (dup_in, dup), (dq_in, dq_any)))
+        for i, (src, dst) in enumerate(((dlat_in, dlat), (dup_in, dup), (dq_in, dq_ref)))
     ]
     for copy in copies:
         copy.start()
@@ -543,7 +546,7 @@
             shape((16, 512), F32), shape((16, 512), F32),
         ),
         in_specs=[anywhere] * 3,
-        out_specs=(anywhere, vmem, vmem, vmem),
+        out_specs=(vmem,) * 4,
         scratch_shapes=[pltpu.VMEM((ROWS, WIDE), BF16), pltpu.VMEM((16, 1024), F32), dma((3,))],
         compiler_params=pltpu.CompilerParams(vmem_limit_bytes=63 * 1024 * 1024),
         name="write_out",

time: 81 us -> 68.6 us (0.85)
  Pallas kernels: 80.2 us -> 67.8 us
    pallas_call x1, Pallas kernels: 13.9 us -> 2.13 us  [shards(): pl.pallas_call(write_out, out_shape=(shape((ROWS, 768), BF16), shape((LAT...]
where the time goes in v4:
time: 68.6 us; the launch traced here: 68.4 us
  Pallas kernels  67.8 us (99%)
    pallas_call x1, Pallas kernels, shards(): pl.pallas_call(kernel, out_shape=(shape((ROWS, 768), BF16), shape((ROWS,...  65.6 us
    pallas_call x1, Pallas kernels, shards(): pl.pallas_call(write_out, out_shape=(shape((ROWS, 768), BF16), shape((LAT...  2.13 us

profile of v4, /device:TPU:1, one launch (start us, length us, event | category | flops | bytes accessed | tf_op | source)
XLA Modules:
  0.0 68.4 jit_solution(9971298976719859014)
XLA Ops:
  0.6 65.6 %mla_backward.1 = (bf16[256,768]{1,0:T(8,128)(2,1)}, bf16[256,640]{1,0:T(8,128)(2,1)}, f32[16,1024]{1,0:T(8,128)}) custom-call(bf16[256,768]{1,0:T(8,128)(2,1)} %q_any.1, bf16[576,256]{1,0:T(8,128)(2,1)} %bitcast.3, bf16[256,512]{1,0:T(8,128)(2,1)} %go_any.1, s32[1,256]{1,0:T(1,128)} %bitcast.4, bf16[512,512]{1,0:T(8,128)(2,1)} %upk_any.1, ...), custom_call_target="tpu_custom_call" | custom-call | tf_op jit(solution)/shard_map/mla_backward/pallas_call | solution.py:483
  66.3 2.1 %write_out.1 = (bf16[256,768]{1,0:T(8,128)(2,1)}, f32[576,256]{1,0:T(8,128)}, f32[16,512]{1,0:T(8,128)}, f32[16,512]{1,0:T(8,128)}) custom-call(bf16[256,768]{1,0:T(8,128)(2,1)} %get-tuple-element.11.dq_in, bf16[256,640]{1,0:T(8,128)(2,1)} %get-tuple-element.12.dlat_in, f32[16,1024]{1,0:T(8,128)} %get-tuple-element.13.dup_in), custom_call_target="tpu_custom_call" | custom-call | tf_op jit(solution)/shard_map/write_out/pallas_call | solution.py:542

commit v5 on v4

--- a/solution.py
+++ b/solution.py
@@ -12,6 +12,7 @@
 ROWS = 256
 HEADS_HERE = 4
 WIDE = 640
+PACK = 144
 SLOTS = 5
 SCALE = (NOPE + ROPE) ** -0.5
 LOG2E = 1.4426950408889634
@@ -27,13 +28,22 @@
     return lax.dot_general(a, b, dims, preferred_element_type=F32)
 
 
+def side_by_side(first, second):
+    return first + pltpu.roll(second, 64, 1)
+
+
+def packed(block):
+    tiles = [block[:, n * 128 : n * 128 + 128] for n in range(4)]
+    return jnp.concatenate(tiles + [side_by_side(block[:16, LAT:], block[16:, LAT:])], axis=0)
+
+
 def kernel(
     q_any, lat_any, go_any, doc_any, upk_any, upv_any,
     dq_any, dlat_any, dup_any,
-    dq_ref, dlat_ref, dup_ref, q_ref, lat_ref, go_ref, doc_ref, win, qx, ups, kv, kxt, latt, probs, gprobs, stats, bias, dqt, dkv,
+    dq_ref, dlat_ref, dup_ref, q_ref, lat_ref, go_ref, docs, win, latent_ref, rope_ref, qx, ups, kv, kxt, latt, probs, gprobs, stats, bias, dqt, dkv,
     part, sib_out, sib_in, ys_out, ys_own, ys_in, own_out, own_in, own_keep,
     g_out, g_in, g_own, gx_out, gx_in, gz_out, gz_in,
-    s_in, s_out, s_z, r_z, s_y, r_y, s_fw, r_fw, s_sib, r_sib, s_ys, r_ys,
+    s_in, s_out, s_doc, r_doc, s_z, r_z, s_y, r_y, s_fw, r_fw, s_sib, r_sib, s_ys, r_ys,
     s_own, r_own, s_ag, r_ag, s_g, r_g, s_gx, r_gx, s_gz, r_gz,
 ):
     dp = lax.axis_index("dp")
@@ -62,7 +72,7 @@
         return (mate, at_ctx(by))
 
     barrier = pltpu.get_barrier_semaphore()
-    senders = [sib, (dp, at_ctx(-2)), (dp, at_ctx(-4))]
+    senders = [sib] + [(dp, at_ctx(-i)) for i in range(1, 5)]
     senders += [owner(by, other) for by in (0, 2, 4) for other in (0, 1) if by or other]
     senders += [at_dp(-i) for i in range(1, 16)]
     senders += [at_x(-i) for i in range(1, 4)]
@@ -73,7 +83,7 @@
     loads = [
         pltpu.make_async_copy(src, dst, s_in.at[i])
         for i, (src, dst) in enumerate((
-            (lat_any, lat_ref), (doc_any, doc_ref), (upk_any, ups.at[:, :512]),
+            (lat_any, lat_ref), (doc_any, docs.at[4, 0:1, :]), (upk_any, ups.at[:, :512]),
             (upv_any, ups.at[:, 512:]), (q_any, q_ref), (go_any, go_ref),
         ))
     ]
@@ -88,19 +98,27 @@
 
     loads[0].wait()
     loads[1].wait()
-    doc_row = doc_ref[...].astype(F32)
+    doc_row = docs[4, 0:1, :]
     line = lax.broadcasted_iota(jnp.int32, (ROWS, ROWS), 0)
     lane = lax.broadcasted_iota(jnp.int32, (ROWS, ROWS), 1)
-    doc_col = jnp.sum(jnp.where(line == lane, doc_row, 0.0), axis=1, keepdims=True)
-    win[4, :, :LAT] = lat_ref[:LAT, :].T
+    rows_of = lat_ref[:LAT, :].T
     tail = jnp.concatenate([lat_ref[LAT:, :].astype(F32), jnp.zeros((64, ROWS), F32)], axis=0).T
-    tail_lane = lax.broadcasted_iota(jnp.int32, (ROWS, 128), 1)
-    win[4, :, LAT:] = jnp.where(tail_lane == 64, doc_col, tail).astype(BF16)
+    for who in range(8):
+        for n in range(4):
+            win[4, who, n * 32 : n * 32 + 32, :] = rows_of[who * 32 : who * 32 + 32, n * 128 : n * 128 + 128]
+        win[4, who, 128:, :] = side_by_side(
+            tail[who * 32 : who * 32 + 16, :], tail[who * 32 + 16 : who * 32 + 32, :]
+        ).astype(BF16)
 
     pl.semaphore_wait(barrier, len(senders))
 
     def shares(slot, who):
-        return win.at[slot, pl.ds(pl.multiple_of(who * 32, 32), 32), :]
+        return win.at[slot, who]
+
+    def tell(by):
+        return remote(
+            docs.at[4], docs.at[4 - by], s_doc.at[by - 1], r_doc.at[by - 1], (dp, at_ctx(by))
+        )
 
     def along_z(index, half):
         who = lax.rem(y + 4 * half, 8)
@@ -112,6 +130,8 @@
     for index in (0, 1):
         for half in (0, 1):
             along_z(index, half).start()
+    for by in range(1, 5):
+        tell(by).start()
 
     fw_own = remote(win.at[4], win.at[3], s_fw.at[0], r_fw.at[0], sib)
     fw_mid = remote(win.at[2], win.at[3], s_fw.at[0], r_fw.at[0], sib)
@@ -122,10 +142,10 @@
     def _():
         fw_own.start()
 
-    passes = ((2, 0), (-2, 0), (1, 0), (-1, 0), (1, 4), (-1, 4))
+    passes = ((2, 0, 0), (-2, 0, 0), (1, 0, 0), (-1, 0, 0), (1, 4, 1), (-1, 4, 1))
 
     def along_y(index, j):
-        by, more = passes[j]
+        by, more, _ = passes[j]
         rows = shares(2 - 2 * index, lax.rem(y + more, 8))
         return remote(rows, rows, s_y.at[index, j], r_y.at[index, j], at_y(by))
 
@@ -142,8 +162,11 @@
     for index in (0, 1):
         for half in (0, 1):
             along_z(index, half).wait_recv()
-        for j in range(6):
-            along_y(index, j).start()
+            for j in range(6):
+                if passes[j][2] == half:
+                    along_y(index, j).start()
+    for by in range(1, 5):
+        tell(by).wait_recv()
 
     def scores(t, carry):
         slot = jnp.where(
@@ -182,9 +205,18 @@
             fw_mid_low.wait_recv()
 
         start = pl.multiple_of(slot * ROWS, ROWS)
-        block = win[slot]
-        latent = block[:, :LAT]
-        rope = block[:, LAT:]
+        for who in range(8):
+            for n in range(4):
+                latent_ref[who * 32 : who * 32 + 32, n * 128 : n * 128 + 128] = win[
+                    slot, who, n * 32 : n * 32 + 32, :
+                ]
+            both_ropes = win[slot, who, 128:, :]
+            rope_ref[who * 32 : who * 32 + 16, :] = both_ropes
+            rope_ref[who * 32 + 16 : who * 32 + 32, :] = pltpu.roll(
+                both_ropes.astype(F32), 64, 1
+            ).astype(BF16)
+        latent = latent_ref[...]
+        rope = rope_ref[...]
         for n in range(4):
             kv[pl.ds(start, ROWS), n * 256 : n * 256 + 256] = mm(
                 latent, ups[:, n * 256 : n * 256 + 256]
@@ -196,9 +228,9 @@
         for g in range(32):
             row = (g % 2) * 256 + (g // 2) * 16
             latt[row : row + 16, pl.ds(start, ROWS)] = flipped[g * 16 : g * 16 + 16, :]
-        docs = rope[:, 64:65].astype(F32)
+        key_docs = jnp.sum(jnp.where(line == lane, docs[slot, 0:1, :], 0), axis=1, keepdims=True)
         past = jnp.logical_or(slot < 4, line <= lane)
-        bias[...] = jnp.where(jnp.logical_and(docs == doc_row, past), 0.0, LOW)
+        bias[...] = jnp.where(jnp.logical_and(key_docs == doc_row, past), 0.0, LOW)
         for h in range(HEADS_HERE):
             cols = slice(h * 256, h * 256 + 256)
             key = kv[pl.ds(start, ROWS), h * 128 : h * 128 + 128]
@@ -227,17 +259,16 @@
     up_high = remote(sib_out.at[1], sib_in.at[1], s_sib.at[1], r_sib.at[1], sib)
 
     def share_of(by):
-        return pl.multiple_of(lax.rem(y + by + 8, 8) * 32, 32)
+        return lax.rem(y + by + 8, 8)
 
     def hop(index, kind, way):
         side = 0 if way > 0 else 1
         by, dest = ((1, 1), (1, 3), (2, 4), (2, 2))[kind]
-        rows, into = pl.ds(share_of(way * dest), 32), pl.ds(0, 32)
+        rows = pl.ds(0, PACK)
         if kind == 2:
-            rows = pl.ds(pl.multiple_of(share_of(4) + 16 * side, 16), 16)
-            into = pl.ds(0, 16)
+            rows = pl.ds(80, 64) if side else pl.ds(0, 80)
         return remote(
-            ys_out.at[index, rows, :], ys_in.at[index, side, kind, into, :],
+            ys_out.at[index, share_of(way * dest), rows, :], ys_in.at[index, side, kind, rows, :],
             s_ys.at[index, side, kind], r_ys.at[index, side, kind], at_y(way * by),
         )
 
@@ -246,12 +277,12 @@
             side = 0 if way > 0 else 1
             hop(index, 1, way).wait_recv()
             hop(index, 2, way).wait_recv()
-            rows = pl.ds(share_of(2 * way), 32)
-            more = ys_in[index, side, 1].astype(F32)
-            half = ys_in[index, side, 2, 0:16, :].astype(F32)
-            empty = jnp.zeros_like(half)
-            more = more + jnp.concatenate([empty, half] if side else [half, empty], axis=0)
-            ys_out[index, rows, :] = (ys_out[index, rows, :].astype(F32) + more).astype(BF16)
+            dest = share_of(2 * way)
+            more = ys_out[index, dest].astype(F32) + ys_in[index, side, 1].astype(F32)
+            rows = slice(80, 144) if side else slice(0, 80)
+            half = more[rows] + ys_in[index, side, 2, rows, :].astype(F32)
+            ys_out[index, dest] = more.astype(BF16)
+            ys_out[index, dest, rows, :] = half.astype(BF16)
             hop(index, 3, way).start()
 
     def grads(t, carry):
@@ -282,8 +313,9 @@
             part[...] += sib_in[which].astype(F32)
 
         def leave(index):
-            ys_out[index] = part[...].astype(BF16)
-            ys_own[index] = part[pl.ds(pl.multiple_of(y * 32, 32), 32), :]
+            for who in range(8):
+                ys_out[index, who] = packed(part[who * 32 : who * 32 + 32, :]).astype(BF16)
+            ys_own[index] = packed(part[pl.ds(pl.multiple_of(y * 32, 32), 32), :])
             for kind in (2, 1, 0):
                 for way in (1, -1):
                     hop(index, kind, way).start()
@@ -307,13 +339,13 @@
             up_low.wait_recv()
             add(0)
             leave(1)
-            relay(0)
 
         @pl.when(t == 4)
         def _():
             up_high.wait_recv()
             add(1)
             leave(2)
+            relay(0)
 
         return carry
 
@@ -357,7 +389,7 @@
         slot = index * 2 + other
         part_of = lax.rem(zl + other, 2)
         return remote(
-            own_out.at[index, pl.ds(pl.multiple_of(part_of * 16, 16), 16), :], own_in.at[slot],
+            own_out.at[index, part_of], own_in.at[slot],
             s_own.at[slot], r_own.at[slot], owner(-4 + 2 * index, other),
         )
 
@@ -368,11 +400,15 @@
             for kind in (0, 3):
                 hop(index, kind, way).wait_recv()
                 here = here + ys_in[index, 0 if way > 0 else 1, kind].astype(F32)
-        own_out[which] = here.astype(BF16)
-
-        @pl.when(which == 2)
-        def _():
-            own_keep[...] = here
+        for half in (0, 1):
+            rope = pltpu.roll(here[128:], 64, 1) if half else here[128:]
+            tiles = [here[n * 32 + half * 16 : n * 32 + half * 16 + 16] for n in range(4)]
+            mine_of = jnp.concatenate(tiles + [rope], axis=0)
+            own_out[which, half] = mine_of.astype(BF16)
+
+            @pl.when(which == 2)
+            def _():
+                own_keep[half] = mine_of
 
         @pl.when(which < 2)
         def _():
@@ -387,11 +423,12 @@
         for other in (0, 1):
             if index < 2 or other:
                 to_owner(index, other).wait_recv()
-    final = own_keep[pl.ds(pl.multiple_of(zl * 16, 16), 16), :]
+    final = own_keep[zl]
     for slot in range(5):
         final = final + own_in[slot if slot < 4 else 5].astype(F32)
     my_rows = pl.ds(pl.multiple_of(dp * 16, 16), 16)
-    dlat_ref[my_rows, :] = final.astype(BF16)
+    for n in range(5):
+        dlat_ref[my_rows, n * 128 : n * 128 + 128] = final[n * 16 : n * 16 + 16].astype(BF16)
 
     def to_all(by):
         return remote(
@@ -437,6 +474,8 @@
             along_z(index, half).wait_send()
         for j in range(6):
             along_y(index, j).wait_send()
+    for by in range(1, 5):
+        tell(by).wait_send()
     fw_own.wait_send()
     fw_mid_low.wait_send()
     for index in range(3):
@@ -492,8 +531,10 @@
             pltpu.VMEM((ROWS, 768), BF16),
             pltpu.VMEM((LAT + ROPE, ROWS), BF16),
             pltpu.VMEM((ROWS, 512), BF16),
-            pltpu.VMEM((1, ROWS), jnp.int32),
-            pltpu.VMEM((SLOTS, ROWS, WIDE), BF16),
+            pltpu.VMEM((SLOTS, 8, ROWS), jnp.int32),
+            pltpu.VMEM((SLOTS, 8, PACK, 128), BF16),
+            pltpu.VMEM((ROWS, LAT), BF16),
+            pltpu.VMEM((ROWS, 128), BF16),
             pltpu.VMEM((ROWS, 1024), BF16),
             pltpu.VMEM((LAT, 1024), BF16),
             pltpu.VMEM((SLOTS * ROWS, 1024), BF16),
@@ -508,12 +549,12 @@
             pltpu.VMEM((ROWS, WIDE), F32),
             pltpu.VMEM((2, ROWS, WIDE), BF16),
             pltpu.VMEM((2, ROWS, WIDE), BF16),
-            pltpu.VMEM((3, ROWS, WIDE), BF16),
-            pltpu.VMEM((3, 32, WIDE), F32),
-            pltpu.VMEM((3, 2, 4, 32, WIDE), BF16),
-            pltpu.VMEM((3, 32, WIDE), BF16),
-            pltpu.VMEM((6, 16, WIDE), BF16),
-            pltpu.VMEM((32, WIDE), F32),
+            pltpu.VMEM((3, 8, PACK, 128), BF16),
+            pltpu.VMEM((3, PACK, 128), F32),
+            pltpu.VMEM((3, 2, 4, PACK, 128), BF16),
+            pltpu.VMEM((3, 2, 80, 128), BF16),
+            pltpu.VMEM((6, 80, 128), BF16),
+            pltpu.VMEM((2, 80, 128), F32),
             pltpu.VMEM((256, 1024), BF16),
             pltpu.VMEM((256, 1024), BF16),
             pltpu.VMEM((256, 1024), F32),
@@ -523,6 +564,7 @@
             pltpu.VMEM((3, 16, 1024), BF16),
             dma((6,)),
             dma((3,)),
+            dma((4,)), dma((4,)),
             dma((2, 2)), dma((2, 2)),
             dma((2, 6)), dma((2, 6)),
             dma((2,)), dma((2,)),

time: 68.6 us -> 65.8 us (0.959)
  Pallas kernels: 67.8 us -> 65 us
    pallas_call x1, Pallas kernels: 65.6 us -> 62.8 us  [shards(): pl.pallas_call(kernel, out_shape=(shape((ROWS, 768), BF16), shape((ROWS,...]
where the time goes in v5:
time: 65.8 us; the launch traced here: 65.6 us
  Pallas kernels  65 us (99%)
    pallas_call x1, Pallas kernels, shards(): pl.pallas_call(kernel, out_shape=(shape((ROWS, 768), BF16), shape((ROWS,...  62.8 us
    pallas_call x1, Pallas kernels, shards(): pl.pallas_call(write_out, out_shape=(shape((ROWS, 768), BF16), shape((LAT...  2.13 us

profile of v5, /device:TPU:1, one launch (start us, length us, event | category | flops | bytes accessed | tf_op | source)
XLA Modules:
  0.0 65.6 jit_solution(1642888401204017082)
XLA Ops:
  0.6 62.8 %mla_backward.1 = (bf16[256,768]{1,0:T(8,128)(2,1)}, bf16[256,640]{1,0:T(8,128)(2,1)}, f32[16,1024]{1,0:T(8,128)}) custom-call(bf16[256,768]{1,0:T(8,128)(2,1)} %q_any.1, bf16[576,256]{1,0:T(8,128)(2,1)} %bitcast.3, bf16[256,512]{1,0:T(8,128)(2,1)} %go_any.1, s32[1,256]{1,0:T(1,128)} %bitcast.4, bf16[512,512]{1,0:T(8,128)(2,1)} %upk_any.1, ...), custom_call_target="tpu_custom_call" | custom-call | tf_op jit(solution)/shard_map/mla_backward/pallas_call | solution.py:522
  63.5 2.1 %write_out.1 = (bf16[256,768]{1,0:T(8,128)(2,1)}, f32[576,256]{1,0:T(8,128)}, f32[16,512]{1,0:T(8,128)}, f32[16,512]{1,0:T(8,128)}) custom-call(bf16[256,768]{1,0:T(8,128)(2,1)} %get-tuple-element.11.dq_in, bf16[256,640]{1,0:T(8,128)(2,1)} %get-tuple-element.12.dlat_in, f32[16,1024]{1,0:T(8,128)} %get-tuple-element.13.dup_in), custom_call_target="tpu_custom_call" | custom-call | tf_op jit(solution)/shard_map/write_out/pallas_call | solution.py:584

commit v6 on v5

--- a/solution.py
+++ b/solution.py
@@ -13,6 +13,7 @@
 HEADS_HERE = 4
 WIDE = 640
 PACK = 144
+HALVES = ((0, 80), (80, 64))
 SLOTS = 5
 SCALE = (NOPE + ROPE) ** -0.5
 LOG2E = 1.4426950408889634
@@ -40,7 +41,7 @@
 def kernel(
     q_any, lat_any, go_any, doc_any, upk_any, upv_any,
     dq_any, dlat_any, dup_any,
-    dq_ref, dlat_ref, dup_ref, q_ref, lat_ref, go_ref, docs, win, latent_ref, rope_ref, qx, ups, kv, kxt, latt, probs, gprobs, stats, bias, dqt, dkv,
+    dq_ref, all_rows, dup_ref, q_ref, lat_ref, go_ref, docs, win, latent_ref, rope_ref, qx, ups, kv, kxt, latt, probs, gprobs, stats, bias, dqt, dkv,
     part, sib_out, sib_in, ys_out, ys_own, ys_in, own_out, own_in, own_keep,
     g_out, g_in, g_own, gx_out, gx_in, gz_out, gz_in,
     s_in, s_out, s_doc, r_doc, s_z, r_z, s_y, r_y, s_fw, r_fw, s_sib, r_sib, s_ys, r_ys,
@@ -51,6 +52,7 @@
     y, zl = lax.div(dp, 2), lax.rem(dp, 2)
     x, zh, core = lax.div(ctx, 8), lax.rem(lax.div(ctx, 2), 4), lax.rem(ctx, 2)
     sib = (dp, ctx + 1 - 2 * core)
+    mate = dp + 1 - 2 * zl
 
     def at_ctx(by):
         return lax.rem(ctx + by + 32, 32)
@@ -68,15 +70,13 @@
         return (dp, x * 8 + lax.rem(zh + by + 4, 4) * 2 + core)
 
     def owner(by, other):
-        mate = dp + 1 - 2 * zl if other else dp
-        return (mate, at_ctx(by))
+        return (mate if other else dp, at_ctx(by))
 
     barrier = pltpu.get_barrier_semaphore()
-    senders = [sib] + [(dp, at_ctx(-i)) for i in range(1, 5)]
-    senders += [owner(by, other) for by in (0, 2, 4) for other in (0, 1) if by or other]
-    senders += [at_dp(-i) for i in range(1, 16)]
+    senders = [(mate, at_ctx(-4)), (dp, at_ctx(-2)), sib, (mate, ctx)]
+    senders += [at_y(by) for by in (-2, 2, -1, 1)]
     senders += [at_x(-i) for i in range(1, 4)]
-    senders += [at_zh(-i) for i in range(1, 4)]
+    senders += [at_zh(-1), at_zh(1)]
     for sender in senders:
         pl.semaphore_signal(barrier, inc=1, device_id=sender, device_id_type=MESH)
 
@@ -115,28 +115,47 @@
     def shares(slot, who):
         return win.at[slot, who]
 
-    def tell(by):
+    def along_ctx(index):
+        return (mate, at_ctx(4)) if index else (dp, at_ctx(2))
+
+    def tell(index):
         return remote(
-            docs.at[4], docs.at[4 - by], s_doc.at[by - 1], r_doc.at[by - 1], (dp, at_ctx(by))
+            docs.at[4], docs.at[2 - 2 * index], s_doc.at[index], r_doc.at[index], along_ctx(index)
         )
 
     def along_z(index, half):
         who = lax.rem(y + 4 * half, 8)
         return remote(
             shares(4, who), shares(2 - 2 * index, who), s_z.at[index, half], r_z.at[index, half],
-            (dp, at_ctx(2 + 2 * index)),
+            along_ctx(index),
         )
 
     for index in (0, 1):
         for half in (0, 1):
             along_z(index, half).start()
-    for by in range(1, 5):
-        tell(by).start()
-
-    fw_own = remote(win.at[4], win.at[3], s_fw.at[0], r_fw.at[0], sib)
-    fw_mid = remote(win.at[2], win.at[3], s_fw.at[0], r_fw.at[0], sib)
-    fw_mid_low = remote(win.at[2], win.at[1], s_fw.at[1], r_fw.at[1], sib)
-    fw_far_low = remote(win.at[0], win.at[1], s_fw.at[1], r_fw.at[1], sib)
+        tell(index).start()
+
+    class Forward:
+        def __init__(self, slot, to, at):
+            self.copies = [
+                remote(win.at[slot], win.at[to], s_fw.at[at], r_fw.at[at], sib),
+                remote(docs.at[slot], docs.at[to], s_fw.at[2 + at], r_fw.at[2 + at], sib),
+            ]
+
+        def start(self):
+            for copy in self.copies:
+                copy.start()
+
+        def wait_recv(self):
+            for copy in self.copies:
+                copy.wait_recv()
+
+        def wait_send(self):
+            for copy in self.copies:
+                copy.wait_send()
+
+    fw_own, fw_mid = Forward(4, 3, 0), Forward(2, 3, 0)
+    fw_mid_low, fw_far_low = Forward(2, 1, 1), Forward(0, 1, 1)
 
     @pl.when(core == 0)
     def _():
@@ -165,8 +184,7 @@
             for j in range(6):
                 if passes[j][2] == half:
                     along_y(index, j).start()
-    for by in range(1, 5):
-        tell(by).wait_recv()
+        tell(index).wait_recv()
 
     def scores(t, carry):
         slot = jnp.where(
@@ -385,13 +403,16 @@
     for by in (2, 1, 3):
         scatter_x(by).start()
 
-    def to_owner(index, other):
-        slot = index * 2 + other
-        part_of = lax.rem(zl + other, 2)
+    def to_owner(index, other, half):
+        slot, rows = index * 2 + other, pl.ds(*HALVES[half])
         return remote(
-            own_out.at[index, part_of], own_in.at[slot],
+            own_out.at[index, rows, :], own_in.at[slot, rows, :],
             s_own.at[slot], r_own.at[slot], owner(-4 + 2 * index, other),
         )
+
+    def by_side(act):
+        for mine_is in (0, 1):
+            pl.when(zl == mine_is)(functools.partial(act, mine_is))
 
     def settle(index):
         which = lax.rem(index + 2 * core, 3)
@@ -400,43 +421,40 @@
             for kind in (0, 3):
                 hop(index, kind, way).wait_recv()
                 here = here + ys_in[index, 0 if way > 0 else 1, kind].astype(F32)
-        for half in (0, 1):
-            rope = pltpu.roll(here[128:], 64, 1) if half else here[128:]
-            tiles = [here[n * 32 + half * 16 : n * 32 + half * 16 + 16] for n in range(4)]
-            mine_of = jnp.concatenate(tiles + [rope], axis=0)
-            own_out[which, half] = mine_of.astype(BF16)
-
-            @pl.when(which == 2)
-            def _():
-                own_keep[half] = mine_of
+        own_out[which] = here.astype(BF16)
+
+        @pl.when(which == 2)
+        def _():
+            own_keep[...] = here
 
         @pl.when(which < 2)
         def _():
-            to_owner(which, 0).start()
-
-        to_owner(which, 1).start()
+            by_side(lambda side: to_owner(which, 0, side).start())
+
+        by_side(lambda side: to_owner(which, 1, 1 - side).start())
 
     for index in range(3):
         settle(index)
 
-    for index in range(3):
-        for other in (0, 1):
-            if index < 2 or other:
-                to_owner(index, other).wait_recv()
-    final = own_keep[zl]
-    for slot in range(5):
-        final = final + own_in[slot if slot < 4 else 5].astype(F32)
-    my_rows = pl.ds(pl.multiple_of(dp * 16, 16), 16)
-    for n in range(5):
-        dlat_ref[my_rows, n * 128 : n * 128 + 128] = final[n * 16 : n * 16 + 16].astype(BF16)
-
-    def to_all(by):
-        return remote(
-            dlat_ref.at[my_rows, :], dlat_ref.at[my_rows, :], s_ag.at[by - 1], r_ag.at[by - 1], at_dp(by)
-        )
-
-    for by in (8, 7, 9, 6, 10, 5, 11, 4, 12, 3, 13, 2, 14, 1, 15):
-        to_all(by).start()
+    pairs = [(index, other) for index in range(3) for other in (0, 1) if index < 2 or other]
+
+    def to_all(by, half):
+        mine_rows = all_rows.at[y, pl.ds(*HALVES[half]), :]
+        return remote(mine_rows, mine_rows, s_ag.at[by - 1], r_ag.at[by - 1], at_dp(by))
+
+    def gather(side):
+        first, count = HALVES[side]
+        rows = slice(first, first + count)
+        for index, other in pairs:
+            to_owner(index, other, side).wait_recv()
+        final = own_keep[rows]
+        for index, other in pairs:
+            final = final + own_in[index * 2 + other, rows, :].astype(F32)
+        all_rows[y, rows, :] = final.astype(BF16)
+        for by in (8, 7, 9, 6, 10, 5, 11, 4, 12, 3, 13, 2, 14, 1, 15):
+            to_all(by, side).start()
+
+    by_side(gather)
 
     for by in range(1, 4):
         scatter_x(by).wait_recv()
@@ -464,9 +482,12 @@
     dup_out = pltpu.make_async_copy(dup_ref, dup_any, s_out.at[1])
     dup_out.start()
 
-    for by in range(1, 16):
-        to_all(by).wait_recv()
-    dlat_out = pltpu.make_async_copy(dlat_ref, dlat_any, s_out.at[2])
+    def gathered(side):
+        for by in range(1, 16):
+            to_all(by, (side + by) % 2).wait_recv()
+
+    by_side(gathered)
+    dlat_out = pltpu.make_async_copy(all_rows, dlat_any, s_out.at[2])
     dlat_out.start()
 
     for index in (0, 1):
@@ -474,8 +495,8 @@
             along_z(index, half).wait_send()
         for j in range(6):
             along_y(index, j).wait_send()
-    for by in range(1, 5):
-        tell(by).wait_send()
+    for index in (0, 1):
+        tell(index).wait_send()
     fw_own.wait_send()
     fw_mid_low.wait_send()
     for index in range(3):
@@ -488,18 +509,20 @@
     for by in range(1, 4):
         scatter_x(by).wait_send()
         scatter_zh(by).wait_send()
-    for index in range(3):
-        for other in (0, 1):
-            if index < 2 or other:
-                to_owner(index, other).wait_send()
-    for by in range(1, 16):
-        to_all(by).wait_send()
+
+    def left(side):
+        for index, other in pairs:
+            to_owner(index, other, (side + other) % 2).wait_send()
+        for by in range(1, 16):
+            to_all(by, side).wait_send()
+
+    by_side(left)
     dq_out.wait()
     dup_out.wait()
     dlat_out.wait()
 
 
-def write_out(dq_in, dlat_in, dup_in, dq_ref, dlat_ref, dupk_ref, dupv_ref, dlat, dup, sem):
+def write_out(dq_in, dlat_in, dup_in, dq_ref, dlat_ref, dupk_ref, dupv_ref, dlat, dup, wide, sem):
     copies = [
         pltpu.make_async_copy(src, dst, sem.at[i])
         for i, (src, dst) in enumerate(((dlat_in, dlat), (dup_in, dup), (dq_in, dq_ref)))
@@ -507,7 +530,13 @@
     for copy in copies:
         copy.start()
     copies[0].wait()
-    dlat_ref[...] = dlat[...].astype(F32).T[: LAT + ROPE, :]
+    for who in range(8):
+        block = dlat[who].astype(F32)
+        for n in range(4):
+            wide[who * 32 : who * 32 + 32, n * 128 : n * 128 + 128] = block[n * 32 : n * 32 + 32]
+        wide[who * 32 : who * 32 + 16, LAT:] = block[128:]
+        wide[who * 32 + 16 : who * 32 + 32, LAT:] = pltpu.roll(block[128:], 64, 1)
+    dlat_ref[...] = wide[...].T[: LAT + ROPE, :]
     copies[1].wait()
     dupk_ref[...] = dup[:, :512]
     dupv_ref[...] = dup[:, 512:]
@@ -521,12 +550,12 @@
     shape = jax.ShapeDtypeStruct
     made = pl.pallas_call(
         kernel,
-        out_shape=(shape((ROWS, 768), BF16), shape((ROWS, WIDE), BF16), shape((16, 1024), F32)),
+        out_shape=(shape((ROWS, 768), BF16), shape((8, PACK, 128), BF16), shape((16, 1024), F32)),
         in_specs=[anywhere] * 6,
         out_specs=(anywhere,) * 3,
         scratch_shapes=[
             pltpu.VMEM((ROWS, 768), BF16),
-            pltpu.VMEM((ROWS, WIDE), BF16),
+            pltpu.VMEM((8, PACK, 128), BF16),
             pltpu.VMEM((16, 1024), F32),
             pltpu.VMEM((ROWS, 768), BF16),
             pltpu.VMEM((LAT + ROPE, ROWS), BF16),
@@ -552,9 +581,9 @@
             pltpu.VMEM((3, 8, PACK, 128), BF16),
             pltpu.VMEM((3, PACK, 128), F32),
             pltpu.VMEM((3, 2, 4, PACK, 128), BF16),
-            pltpu.VMEM((3, 2, 80, 128), BF16),
-            pltpu.VMEM((6, 80, 128), BF16),
-            pltpu.VMEM((2, 80, 128), F32),
+            pltpu.VMEM((3, PACK, 128), BF16),
+            pltpu.VMEM((6, PACK, 128), BF16),
+            pltpu.VMEM((PACK, 128), F32),
             pltpu.VMEM((256, 1024), BF16),
             pltpu.VMEM((256, 1024), BF16),
             pltpu.VMEM((256, 1024), F32),
@@ -564,10 +593,10 @@
             pltpu.VMEM((3, 16, 1024), BF16),
             dma((6,)),
             dma((3,)),
-            dma((4,)), dma((4,)),
+            dma((2,)), dma((2,)),
             dma((2, 2)), dma((2, 2)),
             dma((2, 6)), dma((2, 6)),
-            dma((2,)), dma((2,)),
+            dma((4,)), dma((4,)),
             dma((2,)), dma((2,)),
             dma((3, 2, 4)), dma((3, 2, 4)),
             dma((6,)), dma((6,)),
@@ -589,7 +618,10 @@
         ),
         in_specs=[anywhere] * 3,
         out_specs=(vmem,) * 4,
-        scratch_shapes=[pltpu.VMEM((ROWS, WIDE), BF16), pltpu.VMEM((16, 1024), F32), dma((3,))],
+        scratch_shapes=[
+            pltpu.VMEM((8, PACK, 128), BF16), pltpu.VMEM((16, 1024), F32),
+            pltpu.VMEM((ROWS, WIDE), F32), dma((3,)),
+        ],
         compiler_params=pltpu.CompilerParams(vmem_limit_bytes=63 * 1024 * 1024),
         name="write_out",
     )(*made)

time: 65.8 us -> 62.7 us (0.953)
  the two profiles are of different devices: /device:TPU:1 before, /device:TPU:14 now
where the time goes in v6:
time: 62.7 us; the launch traced here: 62.5 us
  Pallas kernels  61.9 us (99%)
  between operations  0.64 us (1%)
    pallas_call x1, Pallas kernels, shards(): pl.pallas_call(kernel, out_shape=(shape((ROWS, 768), BF16), shape((8, PAC...  59.7 us
    pallas_call x1, Pallas kernels, shards(): pl.pallas_call(write_out, out_shape=(shape((ROWS, 768), BF16), shape((LAT...  2.15 us

profile of v6, /device:TPU:14, one launch (start us, length us, event | category | flops | bytes accessed | tf_op | source)
XLA Modules:
  0.0 62.5 jit_solution(1672525851992995972)
XLA Ops:
  0.6 59.7 %mla_backward.1 = (bf16[256,768]{1,0:T(8,128)(2,1)}, bf16[8,144,128]{2,1,0:T(8,128)(2,1)}, f32[16,1024]{1,0:T(8,128)}) custom-call(bf16[256,768]{1,0:T(8,128)(2,1)} %q_any.1, bf16[576,256]{1,0:T(8,128)(2,1)} %bitcast.3, bf16[256,512]{1,0:T(8,128)(2,1)} %go_any.1, s32[1,256]{1,0:T(1,128)} %bitcast.4, bf16[512,512]{1,0:T(8,128)(2,1)} %upk_any.1, ...), custom_call_target="tpu_custom_call" | custom-call | tf_op jit(solution)/shard_map/mla_backward/pallas_call | solution.py:551
  60.4 2.2 %write_out.1 = (bf16[256,768]{1,0:T(8,128)(2,1)}, f32[576,256]{1,0:T(8,128)}, f32[16,512]{1,0:T(8,128)}, f32[16,512]{1,0:T(8,128)}) custom-call(bf16[256,768]{1,0:T(8,128)(2,1)} %get-tuple-element.11.dq_in, bf16[8,144,128]{2,1,0:T(8,128)(2,1)} %get-tuple-element.12.dlat_in, f32[16,1024]{1,0:T(8,128)} %get-tuple-element.13.dup_in), custom_call_target="tpu_custom_call" | custom-call | tf_op jit(solution)/shard_map/write_out/pallas_call | solution.py:613

commit v7 on v6

--- a/solution.py
+++ b/solution.py
@@ -155,7 +155,11 @@
                 copy.wait_send()
 
     fw_own, fw_mid = Forward(4, 3, 0), Forward(2, 3, 0)
-    fw_mid_low, fw_far_low = Forward(2, 1, 1), Forward(0, 1, 1)
+    fw_mid_low = Forward(2, 1, 1)
+
+    def fw_far(who):
+        remote(win.at[0, who], win.at[1, who], s_fw.at[1], r_fw.at[1], sib).start()
+
 
     @pl.when(core == 0)
     def _():
@@ -186,6 +190,12 @@
                     along_y(index, j).start()
         tell(index).wait_recv()
 
+    @pl.when(core == 1)
+    def _():
+        for half in (0, 1):
+            fw_far(lax.rem(y + 4 * half, 8))
+        remote(docs.at[0], docs.at[1], s_fw.at[3], r_fw.at[3], sib).start()
+
     def scores(t, carry):
         slot = jnp.where(
             t == 0, 4,
@@ -207,12 +217,13 @@
 
         @pl.when(t == 3)
         def _():
-            for j in range(6):
+            for j in (4, 5, 2, 3, 0, 1):
                 along_y(1, j).wait_recv()
-
-            @pl.when(core == 1)
-            def _():
-                fw_far_low.start()
+                by, more, _ = passes[j]
+
+                @pl.when(core == 1)
+                def _():
+                    fw_far(lax.rem(y - by + more + 8, 8))
 
         @pl.when(t == 2 - core)
         def _():
@@ -381,28 +392,6 @@
         g_own[:, n * 256 : n * 256 + 256] = mm(
             latt[pl.ds(mine, 256), :], dkv[:, n * 256 : n * 256 + 256]
         )
-    relay(1)
-    relay(2)
-
-    for h in range(HEADS_HERE):
-        dq = dqt[h].T
-        dq_ref[:, h * 192 : h * 192 + 192] = dq[:, :192].astype(BF16)
-    dq_out = pltpu.make_async_copy(dq_ref, dq_any, s_out.at[0])
-    dq_out.start()
-
-    to_sib.wait_recv()
-    g_own[...] += g_in[...].astype(F32)
-    gx_out[...] = g_own[...].astype(BF16)
-
-    def scatter_x(by):
-        there = pl.multiple_of(lax.rem(x + by, 4) * 64, 64)
-        return remote(
-            gx_out.at[pl.ds(there, 64), :], gx_in.at[by - 1], s_gx.at[by - 1], r_gx.at[by - 1], at_x(by)
-        )
-
-    for by in (2, 1, 3):
-        scatter_x(by).start()
-
     def to_owner(index, other, half):
         slot, rows = index * 2 + other, pl.ds(*HALVES[half])
         return remote(
@@ -433,8 +422,31 @@
 
         by_side(lambda side: to_owner(which, 1, 1 - side).start())
 
-    for index in range(3):
-        settle(index)
+    relay(1)
+    relay(2)
+    settle(0)
+
+    for h in range(HEADS_HERE):
+        dq = dqt[h].T
+        dq_ref[:, h * 192 : h * 192 + 192] = dq[:, :192].astype(BF16)
+    dq_out = pltpu.make_async_copy(dq_ref, dq_any, s_out.at[0])
+    dq_out.start()
+    settle(1)
+
+    to_sib.wait_recv()
+    g_own[...] += g_in[...].astype(F32)
+    gx_out[...] = g_own[...].astype(BF16)
+
+    def scatter_x(by):
+        there = pl.multiple_of(lax.rem(x + by, 4) * 64, 64)
+        return remote(
+            gx_out.at[pl.ds(there, 64), :], gx_in.at[by - 1], s_gx.at[by - 1], r_gx.at[by - 1], at_x(by)
+        )
+
+    for by in (2, 1, 3):
+        scatter_x(by).start()
+
+    settle(2)
 
     pairs = [(index, other) for index in range(3) for other in (0, 1) if index < 2 or other]
 
@@ -451,10 +463,17 @@
         for index, other in pairs:
             final = final + own_in[index * 2 + other, rows, :].astype(F32)
         all_rows[y, rows, :] = final.astype(BF16)
-        for by in (8, 7, 9, 6, 10, 5, 11, 4, 12, 3, 13, 2, 14, 1, 15):
+        for by in (8, 7 + 2 * side, 6, 10, 5, 11, 4, 12, 3, 13, 2, 14, 1, 15):
             to_all(by, side).start()
 
     by_side(gather)
+
+    def pass_on(side):
+        to_all(8, side).wait_recv()
+        piece = all_rows.at[lax.rem(y + 4, 8), pl.ds(*HALVES[side]), :]
+        at = 8 - 2 * side
+        remote(piece, piece, s_ag.at[at], r_ag.at[at], (mate, ctx)).start()
+
 
     for by in range(1, 4):
         scatter_x(by).wait_recv()
@@ -472,6 +491,7 @@
 
     for by in (2, 1, 3):
         scatter_zh(by).start()
+    by_side(pass_on)
 
     for by in range(1, 4):
         scatter_zh(by).wait_recv()
@@ -484,7 +504,8 @@
 
     def gathered(side):
         for by in range(1, 16):
-            to_all(by, (side + by) % 2).wait_recv()
+            if by != 8:
+                to_all(by, (side + by) % 2).wait_recv()
 
     by_side(gathered)
     dlat_out = pltpu.make_async_copy(all_rows, dlat_any, s_out.at[2])

time: 62.7 us -> 62 us (0.989)
  the two profiles are of different devices: /device:TPU:14 before, /device:TPU:1 now
where the time goes in v7:
time: 62 us; the launch traced here: 61.3 us
  Pallas kernels  60.6 us (98%)
  between operations  0.64 us (1%)
    pallas_call x1, Pallas kernels, shards(): pl.pallas_call(kernel, out_shape=(shape((ROWS, 768), BF16), shape((8, PAC...  58.5 us
    pallas_call x1, Pallas kernels, shards(): pl.pallas_call(write_out, out_shape=(shape((ROWS, 768), BF16), shape((LAT...  2.15 us

profile of v7, /device:TPU:1, one launch (start us, length us, event | category | flops | bytes accessed | tf_op | source)
XLA Modules:
  0.0 61.3 jit_solution(11973152814049330319)
XLA Ops:
  0.6 58.5 %mla_backward.1 = (bf16[256,768]{1,0:T(8,128)(2,1)}, bf16[8,144,128]{2,1,0:T(8,128)(2,1)}, f32[16,1024]{1,0:T(8,128)}) custom-call(bf16[256,768]{1,0:T(8,128)(2,1)} %q_any.1, bf16[576,256]{1,0:T(8,128)(2,1)} %bitcast.3, bf16[256,512]{1,0:T(8,128)(2,1)} %go_any.1, s32[1,256]{1,0:T(1,128)} %bitcast.4, bf16[512,512]{1,0:T(8,128)(2,1)} %upk_any.1, ...), custom_call_target="tpu_custom_call" | custom-call | tf_op jit(solution)/shard_map/mla_backward/pallas_call | solution.py:572
  59.1 2.2 %write_out.1 = (bf16[256,768]{1,0:T(8,128)(2,1)}, f32[576,256]{1,0:T(8,128)}, f32[16,512]{1,0:T(8,128)}, f32[16,512]{1,0:T(8,128)}) custom-call(bf16[256,768]{1,0:T(8,128)(2,1)} %get-tuple-element.11.dq_in, bf16[8,144,128]{2,1,0:T(8,128)(2,1)} %get-tuple-element.12.dlat_in, f32[16,1024]{1,0:T(8,128)} %get-tuple-element.13.dup_in), custom_call_target="tpu_custom_call" | custom-call | tf_op jit(solution)/shard_map/write_out/pallas_call | solution.py:634

commit v8 on v7

--- a/solution.py
+++ b/solution.py
@@ -14,6 +14,7 @@
 WIDE = 640
 PACK = 144
 HALVES = ((0, 80), (80, 64))
+PASSED_ON = (2, 6, 3, 5, 4)
 SLOTS = 5
 SCALE = (NOPE + ROPE) ** -0.5
 LOG2E = 1.4426950408889634
@@ -454,6 +455,9 @@
         mine_rows = all_rows.at[y, pl.ds(*HALVES[half]), :]
         return remote(mine_rows, mine_rows, s_ag.at[by - 1], r_ag.at[by - 1], at_dp(by))
 
+    def other_zl(away, side):
+        return (2 * away + 1 - 2 * side) % 16
+
     def gather(side):
         first, count = HALVES[side]
         rows = slice(first, first + count)
@@ -463,16 +467,20 @@
         for index, other in pairs:
             final = final + own_in[index * 2 + other, rows, :].astype(F32)
         all_rows[y, rows, :] = final.astype(BF16)
-        for by in (8, 7 + 2 * side, 6, 10, 5, 11, 4, 12, 3, 13, 2, 14, 1, 15):
-            to_all(by, side).start()
+        for away in (4, 3, 5, 2, 6, 1, 7):
+            to_all(2 * away, side).start()
+            if away not in PASSED_ON:
+                to_all(other_zl(away, side), side).start()
+        to_all(other_zl(0, side), side).start()
 
     by_side(gather)
 
     def pass_on(side):
-        to_all(8, side).wait_recv()
-        piece = all_rows.at[lax.rem(y + 4, 8), pl.ds(*HALVES[side]), :]
-        at = 8 - 2 * side
-        remote(piece, piece, s_ag.at[at], r_ag.at[at], (mate, ctx)).start()
+        for away in PASSED_ON:
+            to_all(2 * away, side).wait_recv()
+            piece = all_rows.at[lax.rem(y + 8 - away, 8), pl.ds(*HALVES[side]), :]
+            at = other_zl(away, side) - 1
+            remote(piece, piece, s_ag.at[at], r_ag.at[at], (mate, ctx)).start()
 
 
     for by in range(1, 4):
@@ -504,7 +512,7 @@
 
     def gathered(side):
         for by in range(1, 16):
-            if by != 8:
+            if by % 2 or by // 2 not in PASSED_ON:
                 to_all(by, (side + by) % 2).wait_recv()
 
     by_side(gathered)

time: 62 us -> 63.1 us (1.018)
  the two profiles are of different devices: /device:TPU:1 before, /device:TPU:64 now
where the time goes in v8:
time: 63.1 us; the launch traced here: 63 us
  Pallas kernels  62.3 us (99%)
  between operations  0.64 us (1%)
    pallas_call x1, Pallas kernels, shards(): pl.pallas_call(kernel, out_shape=(shape((ROWS, 768), BF16), shape((8, PAC...  60.2 us
    pallas_call x1, Pallas kernels, shards(): pl.pallas_call(write_out, out_shape=(shape((ROWS, 768), BF16), shape((LAT...  2.15 us

profile of v8, /device:TPU:64, one launch (start us, length us, event | category | flops | bytes accessed | tf_op | source)
XLA Modules:
  0.0 63.0 jit_solution(17436422904902842606)
XLA Ops:
  0.6 60.2 %mla_backward.1 = (bf16[256,768]{1,0:T(8,128)(2,1)}, bf16[8,144,128]{2,1,0:T(8,128)(2,1)}, f32[16,1024]{1,0:T(8,128)}) custom-call(bf16[256,768]{1,0:T(8,128)(2,1)} %q_any.1, bf16[576,256]{1,0:T(8,128)(2,1)} %bitcast.3, bf16[256,512]{1,0:T(8,128)(2,1)} %go_any.1, s32[1,256]{1,0:T(1,128)} %bitcast.4, bf16[512,512]{1,0:T(8,128)(2,1)} %upk_any.1, ...), custom_call_target="tpu_custom_call" | custom-call | tf_op jit(solution)/shard_map/mla_backward/pallas_call | solution.py:580
  60.8 2.2 %write_out.1 = (bf16[256,768]{1,0:T(8,128)(2,1)}, f32[576,256]{1,0:T(8,128)}, f32[16,512]{1,0:T(8,128)}, f32[16,512]{1,0:T(8,128)}) custom-call(bf16[256,768]{1,0:T(8,128)(2,1)} %get-tuple-element.11.dq_in, bf16[8,144,128]{2,1,0:T(8,128)(2,1)} %get-tuple-element.12.dlat_in, f32[16,1024]{1,0:T(8,128)} %get-tuple-element.13.dup_in), custom_call_target="tpu_custom_call" | custom-call | tf_op jit(solution)/shard_map/write_out/pallas_call | solution.py:642

commit v9 on v7

--- a/solution.py
+++ b/solution.py
@@ -388,6 +388,7 @@
             latt[pl.ds(theirs, 256), :], dkv[:, n * 256 : n * 256 + 256]
         ).astype(BF16)
     to_sib.start()
+    relay(1)
     for n in range(4):
         g_own[:, n * 256 : n * 256 + 256] = mm(
             latt[pl.ds(mine, 256), :], dkv[:, n * 256 : n * 256 + 256]
@@ -422,7 +423,6 @@
 
         by_side(lambda side: to_owner(which, 1, 1 - side).start())
 
-    relay(1)
     relay(2)
     settle(0)
 
@@ -543,13 +543,16 @@
     dlat_out.wait()
 
 
-def write_out(dq_in, dlat_in, dup_in, dq_ref, dlat_ref, dupk_ref, dupv_ref, dlat, dup, wide, sem):
+def write_out(dq_in, dlat_in, dup_in, dq_any, dlat_ref, dupk_ref, dupv_ref, dlat, dup, wide, dq, sem):
     copies = [
         pltpu.make_async_copy(src, dst, sem.at[i])
-        for i, (src, dst) in enumerate(((dlat_in, dlat), (dup_in, dup), (dq_in, dq_ref)))
+        for i, (src, dst) in enumerate(((dlat_in, dlat), (dup_in, dup), (dq_in, dq)))
     ]
     for copy in copies:
         copy.start()
+    dq_out = pltpu.make_async_copy(dq, dq_any, sem.at[3])
+    copies[2].wait()
+    dq_out.start()
     copies[0].wait()
     for who in range(8):
         block = dlat[who].astype(F32)
@@ -561,7 +564,7 @@
     copies[1].wait()
     dupk_ref[...] = dup[:, :512]
     dupv_ref[...] = dup[:, 512:]
-    copies[2].wait()
+    dq_out.wait()
 
 
 def shards(queries, latent, grad_out, doc_ids, up_key, up_value):
@@ -638,10 +641,10 @@
             shape((16, 512), F32), shape((16, 512), F32),
         ),
         in_specs=[anywhere] * 3,
-        out_specs=(vmem,) * 4,
+        out_specs=(anywhere, vmem, vmem, vmem),
         scratch_shapes=[
             pltpu.VMEM((8, PACK, 128), BF16), pltpu.VMEM((16, 1024), F32),
-            pltpu.VMEM((ROWS, WIDE), F32), dma((3,)),
+            pltpu.VMEM((ROWS, WIDE), F32), pltpu.VMEM((ROWS, 768), BF16), dma((4,)),
         ],
         compiler_params=pltpu.CompilerParams(vmem_limit_bytes=63 * 1024 * 1024),
         name="write_out",

time: 62 us -> 62.6 us (level)
  no operation moved by 1% of the time
where the time goes in v9:
time: 62.6 us; the launch traced here: 61.8 us
  Pallas kernels  61.2 us (98%)
  between operations  0.64 us (1%)
    pallas_call x1, Pallas kernels, shards(): pl.pallas_call(kernel, out_shape=(shape((ROWS, 768), BF16), shape((8, PAC...  58.5 us
    pallas_call x1, Pallas kernels, shards(): pl.pallas_call(write_out, out_shape=(shape((ROWS, 768), BF16), shape((LAT...  2.72 us

profile of v9, /device:TPU:1, one launch (start us, length us, event | category | flops | bytes accessed | tf_op | source)
XLA Modules:
  0.0 61.8 jit_solution(16026123791022370443)
XLA Ops:
  0.6 58.5 %mla_backward.1 = (bf16[256,768]{1,0:T(8,128)(2,1)}, bf16[8,144,128]{2,1,0:T(8,128)(2,1)}, f32[16,1024]{1,0:T(8,128)}) custom-call(bf16[256,768]{1,0:T(8,128)(2,1)} %q_any.1, bf16[576,256]{1,0:T(8,128)(2,1)} %bitcast.3, bf16[256,512]{1,0:T(8,128)(2,1)} %go_any.1, s32[1,256]{1,0:T(1,128)} %bitcast.4, bf16[512,512]{1,0:T(8,128)(2,1)} %upk_any.1, ...), custom_call_target="tpu_custom_call" | custom-call | tf_op jit(solution)/shard_map/mla_backward/pallas_call | solution.py:575
  59.1 2.7 %write_out.1 = (bf16[256,768]{1,0:T(8,128)(2,1)}, f32[576,256]{1,0:T(8,128)}, f32[16,512]{1,0:T(8,128)}, f32[16,512]{1,0:T(8,128)}) custom-call(bf16[256,768]{1,0:T(8,128)(2,1)} %get-tuple-element.11.dq_in, bf16[8,144,128]{2,1,0:T(8,128)(2,1)} %get-tuple-element.12.dlat_in, f32[16,1024]{1,0:T(8,128)} %get-tuple-element.13.dup_in), custom_call_target="tpu_custom_call" | custom-call | tf_op jit(solution)/shard_map/write_out/pallas_call | solution.py:637
